TPU v7x, 32 devices: a whole 2x2x4 slice. The times are simulated.
32 devices in a mesh: chan: 4 (over z), sec: 8 (over y, x, core).
Axes of the slice: x: 2, y: 2, z: 4, core: 2. Of those that a mesh axis runs over, the one named last changes fastest.
Arguments:
- psi: bfloat16 [192, 4, 256, 256], P('sec'), may hold values from -6 to 6
- mpo: float32 [4, 4, 4], P('chan'), may hold values from -1.5 to 1.5
- left_env: bfloat16 [4, 64, 256, 256], P('chan', 'sec'), may hold values from -0.375 to 0.375
- right_env: bfloat16 [4, 192, 256, 256], P('chan', 'sec'), may hold values from -0.375 to 0.375
- left_dims: int32 [64], P('sec'), may hold values from 128 to 256, as said below
- right_dims: int32 [192], P('sec'), may hold values from 128 to 256, as said below
- dest_owner: int32 [192, 1], P('sec'), may hold values from 0 to 7, as said below
- left_slot: int32 [192], P('sec'), may hold values from 0 to 7
Outputs:
- h_psi: bfloat16 [192, 4, 256, 256], P('sec', None, 'chan')
Inputs may be any that keep to these rules, and one draw needn't show every extreme that they name: `dest_owner`: each device's 24 blocks name one owner at most 3 times; in every draw some owner is named exactly 3 times by the blocks of every device. `left_dims`: multiples of 128; both bounds are reached. `right_dims`: multiples of 128; both bounds are reached.
All inputs are finite; a program needn't handle non-finite values.
Results may differ from a plain program's by a relative error of at most 0.014.
Values may be sent and summed in bfloat16 or wider, within the bound.
No kernel may reach another device: no remote copies, remote signals or barrier semaphores. Data moves between devices by JAX's collectives and lax.ppermute only.
A program may use at most 192 MiB of HBM per device.

v0:
```python
import jax
import jax.numpy as jnp
from jax import lax
from jax.sharding import PartitionSpec as P


def on_device(psi, mpo, left_env, right_env, left_dims, right_dims, dest_owner, left_slot):
    block_width = psi.shape[2]
    sectors = left_env.shape[1]
    places = jnp.arange(block_width, dtype=jnp.int32)
    right_mask = (places[None, :] < right_dims[:, None]).astype(jnp.bfloat16)
    left_mask = (places[None, :] < left_dims[:, None]).astype(jnp.bfloat16)
    right_kept = right_env[0] * (right_mask[:, :, None] * right_mask[:, None, :])
    left_kept = left_env[0] * (left_mask[:, :, None] * left_mask[:, None, :])
    inner = jnp.einsum("kpac,kdc->kpad", psi, right_kept, preferred_element_type=jnp.float32)
    mixed = jnp.einsum("sp,kpad->ksad", mpo[0], inner, precision=lax.Precision.HIGHEST).astype(
        jnp.bfloat16
    )
    target = dest_owner[:, 0]
    every_env = lax.all_gather(left_kept, "sec", axis=0, tiled=True)
    sector = target * sectors + left_slot
    picked = jnp.take(every_env, sector, axis=0)
    product = jnp.einsum("kea,ksad->ksed", picked, mixed, preferred_element_type=jnp.float32)
    summed = lax.psum_scatter(product.astype(jnp.bfloat16), "chan", scatter_dimension=2, tiled=True)
    return summed


def solution(mesh):
    in_specs = (
        P("sec", None, None, None),
        P("chan", None, None),
        P("chan", "sec", None, None),
        P("chan", "sec", None, None),
        P("sec"),
        P("sec"),
        P("sec", None),
        P("sec"),
    )
    out_specs = P("sec", None, "chan", None)
    return jax.shard_map(
        on_device, mesh=mesh, in_specs=in_specs, out_specs=out_specs, check_vma=False
    )
```

profile of v0, /device:TPU:0, one launch (start us, length us, event | category | flops | bytes accessed | tf_op | source)
XLA Modules:
  0.0 349.3 jit_solution(11758145975981295258)
XLA Ops:
  6.5 0.0 copy-start
  6.5 0.0 copy-start.2
  6.5 0.0 all-gather.2.cloned.1.call-start
  6.5 0.9 fusion.18
  7.4 2.6 bitcast_multiply_fusion.2
  10.0 0.0 all-gather.2.cloned.1.call-update
  10.1 0.0 reduce-scatter.2.cloned.1.call-start
  10.1 0.7 compare_and_fusion
  10.8 0.7 fusion.17
  11.5 0.0 copy-done.2
  11.5 13.7 %fusion.9 = f32[24,256,4,256]{3,1,2,0:T(8,128)} fusion(bf16[24,4,256,256]{3,2,1,0:T(8,128)(2,1)} %param.8, bf16[1,24,256,256]{3,2,1,0:T(8,128)(2,1)S(1)} %copy-done.2, bf16[24,256]{1,0:T(8,128)(2,1)S(1)} %fusion.17), kind=kOutput, calls=%fused_computation.9 | convolution fusion | flops 3230662656 | bytes 40906752 | tf_op jit(solution)/shard_map/kpac,kdc->kpad/dot_general | solution.py:15
  25.2 0.0 copy-done
  25.2 65.4 %fusion = bf16[24,256,256,4]{1,3,2,0:T(4,128)(2,1)} fusion(f32[24,256,4,256]{3,1,2,0:T(8,128)} %fusion.9, f32[1,4,4]{2,1,0:T(4,128)S(1)} %copy-done), kind=kOutput, calls=%fused_computation.1 | convolution fusion | flops 301989888 | bytes 37748800 | tf_op jit(solution)/shard_map/sp,kpad->ksad/dot_general | solution.py:16
  90.7 0.0 all-gather.2.cloned.1.call-done
  90.7 4.1 %gather_fusion = bf16[24,256,256]{2,1,0:T(8,128)(2,1)S(1)} fusion(bf16[64,256,256]{2,1,0:T(8,128)(2,1)} %all-gather.2.cloned.1.call-done, s32[1024]{0:T(1024)S(1)} %pad_clamp_fusion), kind=kCustom, calls=%fused_computation | custom fusion | bytes 6291552 | tf_op jit(solution)/shard_map/jit(_take)/gather | solution.py:22
  94.8 11.0 %convert_bitcast_fusion = bf16[24,4,256,256]{2,3,1,0:T(8,128)(2,1)} fusion(bf16[24,256,256,4]{1,3,2,0:T(4,128)(2,1)} %fusion, bf16[24,256,256]{2,1,0:T(8,128)(2,1)S(1)} %gather_fusion, pred[24]{0:T(512)(128)(4,1)S(1)} %get-tuple-element.5), kind=kOutput, calls=%fused_computation.7 | convolution fusion | flops 3229089792 | bytes 28311576 | tf_op jit(solution)/shard_map/kea,ksad->ksed/dot_general | solution.py:23
  105.8 16.6 %copy.10 = bf16[24,4,256,256]{3,0,1,2:T(8,128)(2,1)} copy(bf16[24,4,256,256]{2,3,1,0:T(8,128)(2,1)} %convert_bitcast_fusion) | data formatting | bytes 25165824 | tf_op jit(solution)/shard_map/convert_element_type | solution.py:24
  122.4 0.0 reduce-scatter.2.cloned.1.call-update
  122.4 0.0 copy-start.1
  122.4 214.7 %reduce-scatter.2.cloned.1.call-done = bf16[24,4,64,256]{3,0,1,2:T(8,128)(2,1)} async-done(((bf16[24,4,256,256]{3,0,1,2:T(8,128)(2,1)}), bf16[24,4,64,256]{3,0,1,2:T(8,128)(2,1)}) %reduce-scatter.2.cloned.1.call-update) | async-done | bytes 3145744 | tf_op jit(solution)/shard_map/reduce_scatter | solution.py:24
  337.1 5.3 %copy.11 = bf16[24,4,64,256]{3,2,1,0:T(8,128)(2,1)} copy(bf16[24,4,64,256]{3,0,1,2:T(8,128)(2,1)} %reduce-scatter.2.cloned.1.call-done) | data formatting | bytes 6291456 | tf_op jit(solution)/shard_map/reduce_scatter | solution.py:24
  342.5 0.0 copy-done.1
  (1 shorter events, 0.0 us)
Async XLA Ops:
  6.5 18.7 %copy-start = (f32[1,4,4]{2,1,0:T(4,128)S(1)}, f32[1,4,4]{2,1,0:T(4,128)}, u32[]{:S(2)}) copy-start(f32[1,4,4]{2,1,0:T(4,128)} %param.9) | copy-start | bytes 196
  6.5 5.0 %copy-start.2 = (bf16[1,24,256,256]{3,2,1,0:T(8,128)(2,1)S(1)}, bf16[1,24,256,256]{3,2,1,0:T(8,128)(2,1)}, u32[]{:S(2)}) copy-start(bf16[1,24,256,256]{3,2,1,0:T(8,128)(2,1)} %param.11) | copy-start | bytes 9437188
  6.5 84.1 %all-gather.2.cloned.1.call-start = ((), (), s32[]{:S(2)}) async-start(), calls=%async_computation.1 | async-start | bytes 9437184 | tf_op jit(solution)/shard_map/all_gather | solution.py:20
  10.1 327.1 %reduce-scatter.2.cloned.1.call-start = ((), (), s32[]{:S(2)}) async-start(), calls=%async_computation.2 | async-start | bytes 15728640 | tf_op jit(solution)/shard_map/reduce_scatter | solution.py:24
  122.4 220.0 %copy-start.1 = (f32[1,4,4]{2,1,0:T(4,128)S(1)}, f32[1,4,4]{2,1,0:T(4,128)}, u32[]{:S(2)}) copy-start(f32[1,4,4]{2,1,0:T(4,128)} %param.9) | copy-start | bytes 196
Sparse Core Ops, SparseCore 0:
  10.2 57.1 all-gather.1
  122.5 214.5 reduce-scatter.1
where the time goes:
time: 350 us; the launch traced here: 349 us
  waiting for transfers between devices  215 us (61%)
  matrix products  90.1 us (26%)
  local copies, waits for them, and re-layouts  26.1 us (7%)
  between operations  13.4 us (4%)
  other arithmetic  4.92 us (1%)
    reduce_scatter x1, waiting for transfers between devices, on_device(): lax.psum_scatter(product.astype(jnp.bfloat16), 'chan', scatter_dimension=...  215 us
    dot_general x1, matrix products, on_device(): jnp.einsum('sp,kpad->ksad', mpo[0], inner, precision=lax.Precision.HIGHEST)  65.4 us
    convert_element_type x1, local copies, waits for them, and re-layouts, on_device(): product.astype(jnp.bfloat16)  16.6 us
    dot_general x1, matrix products, on_device(): jnp.einsum('kpac,kdc->kpad', psi, right_kept, preferred_element_type=jnp....  13.7 us
    dot_general x1, matrix products, on_device(): jnp.einsum('kea,ksad->ksed', picked, mixed, preferred_element_type=jnp.fl...  11 us
  transfers between devices with their start and end apart: 2, of which 1 were waited for; matrix products, arithmetic and copies ran while one was open for 23% of the time, Pallas kernels for 0%

commit v1 on v0

v1 whole, which is shorter than its diff:
```python
import functools

import jax
import jax.numpy as jnp
from jax import lax
from jax.experimental import pallas as pl
from jax.experimental.pallas import tpu as pltpu
from jax.sharding import PartitionSpec as P


def block_kernel(hi, rows, sector, right_dims, mpo, psi, left, own_right, *rest):
    other_rights = rest[: hi - 1]
    keep, send = rest[hi - 1 :]
    k = pl.program_id(0)
    states, width = psi.shape[1], psi.shape[2]
    stacked = left[0]
    parts = [
        jnp.dot(stacked, psi[0, p], preferred_element_type=jnp.float32) for p in range(states)
    ]
    r = right_dims[k]
    total = None
    for i in range(hi):
        right = own_right[0] if i == 0 else other_rights[i - 1][0]
        inside = (lax.broadcasted_iota(jnp.int32, right.shape, 0) < r) & (
            lax.broadcasted_iota(jnp.int32, right.shape, 1) < r
        )
        right = jnp.where(inside, right, jnp.zeros_like(right))
        mixed = []
        for s in range(states):
            acc = None
            for p in range(states):
                piece = parts[p][i * rows : (i + 1) * rows] * mpo[i, s * states + p]
                acc = piece if acc is None else acc + piece
            mixed.append(acc.astype(jnp.bfloat16))
        mixed = jnp.concatenate(mixed, axis=0)
        product = lax.dot_general(
            mixed, right, (((1,), (1,)), ((), ())), preferred_element_type=jnp.float32
        )
        total = product if total is None else total + product
    own = keep.shape[2]
    for s in range(states):
        keep[0, s] = total[s * rows : s * rows + own].astype(keep.dtype)
        send[0, :, s] = (
            total[s * rows + own : (s + 1) * rows].reshape(-1, own, width).astype(send.dtype)
        )


def blocks_call(first, count, hi, lo, own_rows, sector, right_dims, mpo, psi, left, own_right, others):
    states, width = psi.shape[1], psi.shape[2]
    rows = lo * own_rows
    grid_spec = pltpu.PrefetchScalarGridSpec(
        num_scalar_prefetch=3,
        grid=(count,),
        in_specs=[
            pl.BlockSpec((1, states, width, width), lambda k, sec, *_: (k + first, 0, 0, 0)),
            pl.BlockSpec((1, hi * rows, width), lambda k, sec, *_: (sec[k], 0, 0)),
            pl.BlockSpec((1, width, width), lambda k, *_: (k + first, 0, 0)),
        ]
        + [pl.BlockSpec((1, width, width), lambda k, *_: (k, 0, 0))] * (hi - 1),
        out_specs=[
            pl.BlockSpec((1, states, own_rows, width), lambda k, *_: (k, 0, 0, 0)),
            pl.BlockSpec((1, lo - 1, states, own_rows, width), lambda k, *_: (k, 0, 0, 0, 0)),
        ],
    )
    unit = states * width * width
    return pl.pallas_call(
        functools.partial(block_kernel, hi, rows),
        grid_spec=grid_spec,
        out_shape=[
            jax.ShapeDtypeStruct((count, states, own_rows, width), jnp.bfloat16),
            jax.ShapeDtypeStruct((count, lo - 1, states, own_rows, width), jnp.bfloat16),
        ],
        compiler_params=pltpu.CompilerParams(vmem_limit_bytes=48 * 2**20),
        cost_estimate=pl.CostEstimate(
            flops=count * 4 * hi * rows * unit,
            bytes_accessed=count * 5 * unit,
            transcendentals=0,
        ),
    )(sector, right_dims, mpo, psi, left, own_right, *others)


def on_device(n_chan, psi, mpo, left_env, right_env, left_dims, right_dims, dest_owner, left_slot):
    blocks, states, width = psi.shape[:3]
    sectors = left_env.shape[1]
    hi = 2 if n_chan % 2 == 0 else 1
    lo = n_chan // hi
    own_rows = width // n_chan
    here = lax.axis_index("chan")
    h, l = here // lo, here % lo

    def over_hi(x, i):
        pairs = [(c, ((c // lo + i) % hi) * lo + c % lo) for c in range(n_chan)]
        return lax.ppermute(x, "chan", pairs)

    def over_lo(x, j):
        pairs = [(c, (c // lo) * lo + (c % lo + j) % lo) for c in range(n_chan)]
        return lax.ppermute(x, "chan", pairs)

    chunks = 6 if blocks % 6 == 0 else 1
    count = blocks // chunks
    right = right_env[0]
    moved = []
    for m in range(chunks):
        piece = right[m * count : (m + 1) * count]
        if m >= 2:
            piece, _ = lax.optimization_barrier((piece, moved[m - 2]))
        moved.append([over_hi(piece, i) for i in range(1, hi)])

    places = jnp.arange(width, dtype=jnp.int32)
    left_mask = (places[None, :] < left_dims[:, None]).astype(jnp.bfloat16)
    left_kept = left_env[0] * (left_mask[:, :, None] * left_mask[:, None, :])
    left_kept = left_kept.reshape(sectors, hi, lo, own_rows, width)
    left_kept = jnp.take(left_kept, (l + jnp.arange(lo)) % lo, axis=2)

    def for_half(i):
        return lax.dynamic_index_in_dim(left_kept, (h + i) % hi, axis=1, keepdims=False)

    lefts = [for_half(0)] + [over_hi(for_half(i), i) for i in range(1, hi)]
    mpos = [mpo[0]] + [over_hi(mpo[0], i) for i in range(1, hi)]
    mpo_all = jnp.stack(mpos).reshape(hi, states * states)
    stacked = jnp.stack(lefts, axis=1).reshape(sectors, hi * lo * own_rows, width)
    every = lax.all_gather(stacked, "sec", axis=0, tiled=True)

    sector = dest_owner[:, 0] * sectors + left_slot
    outs = []
    for m in range(chunks):
        span = slice(m * count, (m + 1) * count)
        keep, send = blocks_call(
            m * count, count, hi, lo, own_rows, sector[span], right_dims[span], mpo_all,
            psi, every, right, moved[m],
        )
        total = keep.astype(jnp.float32)
        for j in range(1, lo):
            total = total + over_lo(send[:, j - 1], j).astype(jnp.float32)
        outs.append(total.astype(jnp.bfloat16))
    return jnp.concatenate(outs, axis=0)


def solution(mesh):
    in_specs = (
        P("sec", None, None, None),
        P("chan", None, None),
        P("chan", "sec", None, None),
        P("chan", "sec", None, None),
        P("sec"),
        P("sec"),
        P("sec", None),
        P("sec"),
    )
    out_specs = P("sec", None, "chan", None)
    return jax.shard_map(
        functools.partial(on_device, mesh.shape["chan"]),
        mesh=mesh,
        in_specs=in_specs,
        out_specs=out_specs,
        check_vma=False,
    )
```

time: 350 us -> 251 us (0.72)
  matrix products: 90.1 us -> 0 us
  waiting for transfers between devices: 215 us -> 178 us
  Pallas kernels: 0 us -> 29.7 us
  local copies, waits for them, and re-layouts: 26.1 us -> 9.21 us
  starting transfers between devices: 0.04 us -> 14.5 us
    reduce_scatter x1 -> x0, waiting for transfers between devices: 215 us -> none  [on_device(): lax.psum_scatter(product.astype(jnp.bfloat16), 'chan', scatter_dimension=...]
    ppermute x0 -> x14, waiting for transfers between devices: none -> 178 us  [the longest x8 136 us: over_hi(): return lax.ppermute(x, 'chan', pairs)]
    dot_general x3 -> x0, matrix products: 90.1 us -> none  [the longest x1 65.4 us: on_device(): jnp.einsum('sp,kpad->ksad', mpo[0], inner, precision=lax.Precision.HIGHEST)]
    pallas_call x0 -> x6, Pallas kernels: none -> 29.7 us  [blocks_call(): pl.pallas_call(functools.partial(block_kernel, hi, rows), grid_spec=grid_...]
    convert_element_type x1 -> x0, local copies, waits for them, and re-layouts: 16.6 us -> none  [on_device(): product.astype(jnp.bfloat16)]
    ppermute x0 -> x14, starting transfers between devices: none -> 14.5 us  [the longest x8 9.96 us: over_hi(): return lax.ppermute(x, 'chan', pairs)]
    unnamed x6 -> x28, local copies, waits for them, and re-layouts: 0.01 us -> 5.94 us
    reduce_scatter x1 -> x0, local copies, waits for them, and re-layouts: 5.32 us -> none  [on_device(): lax.psum_scatter(product.astype(jnp.bfloat16), 'chan', scatter_dimension=...]
  transfers between devices with their start and end apart: 2 -> 15, of which waited for: 1 -> 9; matrix products, arithmetic and copies ran while one was open for 23% -> 1% of each run, Pallas kernels for 0% -> 12%
where the time goes in v1:
time: 251 us; the launch traced here: 250 us
  waiting for transfers between devices  178 us (71%)
  Pallas kernels  29.7 us (12%)
  starting transfers between devices  14.5 us (6%)
  between operations  13.7 us (5%)
  local copies, waits for them, and re-layouts  9.21 us (4%)
  other arithmetic  5.1 us (2%)
    ppermute x8, waiting for transfers between devices, over_hi(): return lax.ppermute(x, 'chan', pairs)  136 us
    ppermute x6, waiting for transfers between devices, over_lo(): return lax.ppermute(x, 'chan', pairs)  42 us
    pallas_call x6, Pallas kernels, blocks_call(): pl.pallas_call(functools.partial(block_kernel, hi, rows), grid_spec=grid_...  29.7 us
    ppermute x8, starting transfers between devices, over_hi(): return lax.ppermute(x, 'chan', pairs)  9.96 us
    unnamed x28, local copies, waits for them, and re-layouts  5.94 us
  transfers between devices with their start and end apart: 15, of which 9 were waited for; matrix products, arithmetic and copies ran while one was open for 1% of the time, Pallas kernels for 12%

profile of v1, /device:TPU:0, one launch (start us, length us, event | category | flops | bytes accessed | tf_op | source)
XLA Modules:
  0.0 250.3 jit_solution(17979441613213548258)
XLA Ops:
  8.1 1.6 multiply_multiply_fusion
  10.6 4.1 %collective-permute-start.1 = (bf16[8,2,64,256]{3,2,0,1:T(8,128)(2,1)S(1)}, bf16[8,2,64,256]{3,2,0,1:T(8,128)(2,1)S(1)}, u32[]{:S(2)}, u32[]{:S(2)}) collective-permute-start(bf16[8,2,64,256]{3,2,0,1:T(8,128)(2,1)S(1)} %get-tuple-element.44), channel_id=1, source_target_pairs={{0,16},{8,24},{16,0},{24,8},{1,17},{9,25},{17,1},{25,9},{2,18},{10... | collective-permute-start | bytes 1572872 | tf_op jit(solution)/shard_map/ppermute | solution.py:93
  14.7 23.2 %collective-permute-done.1 = bf16[8,2,64,256]{3,2,0,1:T(8,128)(2,1)S(1)} collective-permute-done((bf16[8,2,64,256]{3,2,0,1:T(8,128)(2,1)S(1)}, bf16[8,2,64,256]{3,2,0,1:T(8,128)(2,1)S(1)}, u32[]{:S(2)}, u32[]{:S(2)}) %collective-permute-start.1) | collective-permute-done | bytes 524320 | tf_op jit(solution)/shard_map/ppermute | solution.py:93
  37.9 1.0 copy.14
  39.1 1.3 slice_bitcast_fusion
  40.3 2.9 %collective-permute-start.2 = (bf16[4,256,256]{2,1,0:T(8,128)(2,1)S(1)}, bf16[4,256,256]{2,1,0:T(8,128)(2,1)S(1)}, u32[]{:S(2)}, u32[]{:S(2)}) collective-permute-start(bf16[4,256,256]{2,1,0:T(8,128)(2,1)S(1)} %get-tuple-element.41), channel_id=1, source_target_pairs={{0,16},{8,24},{16,0},{24,8},{1,17},{9,25},{17,1},{25,9},{2,18},{10... | collective-permute-start | bytes 1572872 | tf_op jit(solution)/shard_map/ppermute | solution.py:93
  43.2 35.3 %collective-permute-done.4.rest_0_ = bf16[4,256,256]{2,1,0:T(8,128)(2,1)S(1)} collective-permute-done((bf16[4,256,256]{2,1,0:T(8,128)(2,1)S(1)}, bf16[4,256,256]{2,1,0:T(8,128)(2,1)S(1)}, u32[]{:S(2)}, u32[]{:S(2)}) %collective-permute-start.4) | collective-permute-done | bytes 524320 | tf_op jit(solution)/shard_map/ppermute | solution.py:93
  79.4 21.6 %collective-permute-done.2.rest_0_ = bf16[4,256,256]{2,1,0:T(8,128)(2,1)S(1)} collective-permute-done((bf16[4,256,256]{2,1,0:T(8,128)(2,1)S(1)}, bf16[4,256,256]{2,1,0:T(8,128)(2,1)S(1)}, u32[]{:S(2)}, u32[]{:S(2)}) %collective-permute-start.2) | collective-permute-done | bytes 524320 | tf_op jit(solution)/shard_map/ppermute | solution.py:93
  101.8 2.9 %collective-permute-start = (f32[4,4]{1,0:T(4,128)S(1)}, f32[4,4]{1,0:T(4,128)S(1)}, u32[]{:S(2)}, u32[]{:S(2)}) collective-permute-start(f32[4,4]{1,0:T(4,128)S(1)} %bitcast.50), channel_id=1, source_target_pairs={{0,16},{8,24},{16,0},{24,8},{1,17},{9,25},{17,1},{25,9},{2,18},{10... | collective-permute-start | bytes 200 | tf_op jit(solution)/shard_map/ppermute | solution.py:93
  104.7 18.8 %collective-permute-done.8.rest_0_ = bf16[4,256,256]{2,1,0:T(8,128)(2,1)S(1)} collective-permute-done((bf16[4,256,256]{2,1,0:T(8,128)(2,1)S(1)}, bf16[4,256,256]{2,1,0:T(8,128)(2,1)S(1)}, u32[]{:S(2)}, u32[]{:S(2)}) %collective-permute-start.8) | collective-permute-done | bytes 524320 | tf_op jit(solution)/shard_map/ppermute | solution.py:93
  124.3 21.7 %collective-permute-done.6.rest_0_ = bf16[4,256,256]{2,1,0:T(8,128)(2,1)S(1)} collective-permute-done((bf16[4,256,256]{2,1,0:T(8,128)(2,1)S(1)}, bf16[4,256,256]{2,1,0:T(8,128)(2,1)S(1)}, u32[]{:S(2)}, u32[]{:S(2)}) %collective-permute-start.6) | collective-permute-done | bytes 524320 | tf_op jit(solution)/shard_map/ppermute | solution.py:93
  148.1 4.9 %shard_map.82 = (bf16[4,4,64,256]{3,2,1,0:T(8,128)(2,1)S(1)}, bf16[4,1,4,64,256]{4,3,2,1,0:T(8,128)(2,1)S(1)}) custom-call(s32[4]{0:T(128)S(1)} %get-tuple-element.57.sector, s32[4]{0:T(128)S(1)} %get-tuple-element.49.right_dims, f32[2,16]{1,0:T(2,128)S(1)} %pad_maximum_fusion.1.mpo, bf16[24,4,256,256]{3,2,1,0:T(8,128)(2,1)} %psi.11, ...), custom_call_target="tpu_custom_call" | custom-call | flops 1073741824 | bytes 5242880 | tf_op jit(solution)/shard_map/pallas_call | solution.py:66
  153.2 15.5 %collective-permute-done.12.rest_0_ = bf16[4,256,256]{2,1,0:T(8,128)(2,1)} collective-permute-done((bf16[4,256,256]{2,1,0:T(8,128)(2,1)}, bf16[4,256,256]{2,1,0:T(8,128)(2,1)}, u32[]{:S(2)}, u32[]{:S(2)}) %collective-permute-start.12) | collective-permute-done | bytes 524320 | tf_op jit(solution)/shard_map/ppermute | solution.py:93
  168.7 5.0 %shard_map.87 = (bf16[4,4,64,256]{3,2,1,0:T(8,128)(2,1)S(1)}, bf16[4,1,4,64,256]{4,3,2,1,0:T(8,128)(2,1)S(1)}) custom-call(s32[4]{0:T(128)S(1)} %get-tuple-element.62.sector, s32[4]{0:T(128)S(1)} %get-tuple-element.45.right_dims, f32[2,16]{1,0:T(2,128)S(1)} %pad_maximum_fusion.1.mpo, bf16[24,4,256,256]{3,2,1,0:T(8,128)(2,1)} %psi.11, ...), custom_call_target="tpu_custom_call" | custom-call | flops 1073741824 | bytes 5242880 | tf_op jit(solution)/shard_map/pallas_call | solution.py:66
  173.8 4.9 %shard_map.83 = (bf16[4,4,64,256]{3,2,1,0:T(8,128)(2,1)S(1)}, bf16[4,1,4,64,256]{4,3,2,1,0:T(8,128)(2,1)S(1)}) custom-call(s32[4]{0:T(128)S(1)} %get-tuple-element.58.sector, s32[4]{0:T(128)S(1)} %get-tuple-element.48.right_dims, f32[2,16]{1,0:T(2,128)S(1)} %pad_maximum_fusion.1.mpo, bf16[24,4,256,256]{3,2,1,0:T(8,128)(2,1)} %psi.11, ...), custom_call_target="tpu_custom_call" | custom-call | flops 1073741824 | bytes 5242880 | tf_op jit(solution)/shard_map/pallas_call | solution.py:66
  178.8 2.1 collective-permute-start.5
  180.8 5.0 %shard_map.86 = (bf16[4,4,64,256]{3,2,1,0:T(8,128)(2,1)S(1)}, bf16[4,1,4,64,256]{4,3,2,1,0:T(8,128)(2,1)S(1)}) custom-call(s32[4]{0:T(128)S(1)} %get-tuple-element.61.sector, s32[4]{0:T(128)S(1)} %get-tuple-element.50.right_dims, f32[2,16]{1,0:T(2,128)S(1)} %pad_maximum_fusion.1.mpo, bf16[24,4,256,256]{3,2,1,0:T(8,128)(2,1)} %psi.11, ...), custom_call_target="tpu_custom_call" | custom-call | flops 1073741824 | bytes 5242880 | tf_op jit(solution)/shard_map/pallas_call | solution.py:66
  186.0 4.9 %shard_map.84 = (bf16[4,4,64,256]{3,2,1,0:T(8,128)(2,1)S(1)}, bf16[4,1,4,64,256]{4,3,2,1,0:T(8,128)(2,1)S(1)}) custom-call(s32[4]{0:T(128)S(1)} %get-tuple-element.59.sector, s32[4]{0:T(128)S(1)} %get-tuple-element.47.right_dims, f32[2,16]{1,0:T(2,128)S(1)} %pad_maximum_fusion.1.mpo, bf16[24,4,256,256]{3,2,1,0:T(8,128)(2,1)} %psi.11, ...), custom_call_target="tpu_custom_call" | custom-call | flops 1073741824 | bytes 5242880 | tf_op jit(solution)/shard_map/pallas_call | solution.py:66
  190.9 2.1 collective-permute-start.7
  192.9 4.9 %shard_map.85 = (bf16[4,4,64,256]{3,2,1,0:T(8,128)(2,1)S(1)}, bf16[4,1,4,64,256]{4,3,2,1,0:T(8,128)(2,1)S(1)}) custom-call(s32[4]{0:T(128)S(1)} %get-tuple-element.60.sector, s32[4]{0:T(128)S(1)} %get-tuple-element.46.right_dims, f32[2,16]{1,0:T(2,128)S(1)} %pad_maximum_fusion.1.mpo, bf16[24,4,256,256]{3,2,1,0:T(8,128)(2,1)} %psi.11, ...), custom_call_target="tpu_custom_call" | custom-call | flops 1073741824 | bytes 5242880 | tf_op jit(solution)/shard_map/pallas_call | solution.py:66
  198.1 11.6 %collective-permute-done.5 = bf16[4,4,64,256]{3,2,1,0:T(8,128)(2,1)S(1)} collective-permute-done((bf16[4,4,64,256]{3,2,1,0:T(8,128)(2,1)S(1)}, bf16[4,4,64,256]{3,2,1,0:T(8,128)(2,1)S(1)}, u32[]{:S(2)}, u32[]{:S(2)}) %collective-permute-start.5) | collective-permute-done | bytes 524320 | tf_op jit(solution)/shard_map/ppermute | solution.py:97
  209.9 22.3 %collective-permute-done.7 = bf16[4,4,64,256]{3,2,1,0:T(8,128)(2,1)S(1)} collective-permute-done((bf16[4,4,64,256]{3,2,1,0:T(8,128)(2,1)S(1)}, bf16[4,4,64,256]{3,2,1,0:T(8,128)(2,1)S(1)}, u32[]{:S(2)}, u32[]{:S(2)}) %collective-permute-start.7) | collective-permute-done | bytes 524320 | tf_op jit(solution)/shard_map/ppermute | solution.py:97
  232.4 8.0 %collective-permute-done.9 = bf16[4,4,64,256]{3,2,1,0:T(8,128)(2,1)S(1)} collective-permute-done((bf16[4,4,64,256]{3,2,1,0:T(8,128)(2,1)S(1)}, bf16[4,4,64,256]{3,2,1,0:T(8,128)(2,1)S(1)}, u32[]{:S(2)}, u32[]{:S(2)}) %collective-permute-start.9) | collective-permute-done | bytes 524320 | tf_op jit(solution)/shard_map/ppermute | solution.py:97
  240.8 1.6 copy-done.9
  (65 shorter events, 9.3 us)
Async XLA Ops:
  6.5 140.5 %all-gather.2.cloned.1.call-start = ((), (), s32[]{:S(2)}) async-start(), calls=%async_computation | async-start | bytes 9437184 | tf_op jit(solution)/shard_map/all_gather | solution.py:122
  10.6 28.4 %copy-start = (bf16[1,24,256,256]{3,2,1,0:T(8,128)(2,1)S(1)}, bf16[1,24,256,256]{3,2,1,0:T(8,128)(2,1)}, u32[]{:S(2)}) copy-start(bf16[1,24,256,256]{3,2,1,0:T(8,128)(2,1)} %param.11) | copy-start | bytes 9437188
  10.6 27.3 %collective-permute-start.1 = (bf16[8,2,64,256]{3,2,0,1:T(8,128)(2,1)S(1)}, bf16[8,2,64,256]{3,2,0,1:T(8,128)(2,1)S(1)}, u32[]{:S(2)}, u32[]{:S(2)}) collective-permute-start(bf16[8,2,64,256]{3,2,0,1:T(8,128)(2,1)S(1)} %get-tuple-element.44), channel_id=1, source_target_pairs={{0,16},{8,24},{16,0},{24,8},{1,17},{9,25},{17,1},{25,9},{2,18},{10... | collective-permute-start | bytes 1572872 | tf_op jit(solution)/shard_map/ppermute | solution.py:93
  39.0 62.8 %copy-start.11 = (f32[1,4,4]{2,1,0:T(4,128)S(1)}, f32[1,4,4]{2,1,0:T(4,128)}, u32[]{:S(2)}) copy-start(f32[1,4,4]{2,1,0:T(4,128)} %param.9) | copy-start | bytes 196
  39.0 85.3 %copy-start.12 = (s32[24]{0:T(128)S(1)}, s32[24]{0:T(128)}, u32[]{:S(2)}) copy-start(s32[24]{0:T(128)} %param.15) | copy-start | bytes 292
  39.0 85.3 %copy-start.13 = (s32[24,1]{0,1:T(1,128)S(1)}, s32[24,1]{0,1:T(1,128)}, u32[]{:S(2)}) copy-start(s32[24,1]{0,1:T(1,128)} %param.14) | copy-start | bytes 292
  39.0 107.8 %copy-start.10 = (s32[24]{0:T(128)S(1)}, s32[24]{0:T(128)}, u32[]{:S(2)}) copy-start(s32[24]{0:T(128)} %param.13) | copy-start | bytes 292
  40.3 38.2 %collective-permute-start.4 = (bf16[4,256,256]{2,1,0:T(8,128)(2,1)S(1)}, bf16[4,256,256]{2,1,0:T(8,128)(2,1)S(1)}, u32[]{:S(2)}, u32[]{:S(2)}) collective-permute-start(bf16[4,256,256]{2,1,0:T(8,128)(2,1)S(1)} %get-tuple-element.40), channel_id=1, source_target_pairs={{0,16},{8,24},{16,0},{24,8},{1,17},{9,25},{17,1},{25,9},{2,18},{10... | collective-permute-start | bytes 1572872 | tf_op jit(solution)/shard_map/ppermute | solution.py:93
  40.3 60.7 %collective-permute-start.2 = (bf16[4,256,256]{2,1,0:T(8,128)(2,1)S(1)}, bf16[4,256,256]{2,1,0:T(8,128)(2,1)S(1)}, u32[]{:S(2)}, u32[]{:S(2)}) collective-permute-start(bf16[4,256,256]{2,1,0:T(8,128)(2,1)S(1)} %get-tuple-element.41), channel_id=1, source_target_pairs={{0,16},{8,24},{16,0},{24,8},{1,17},{9,25},{17,1},{25,9},{2,18},{10... | collective-permute-start | bytes 1572872 | tf_op jit(solution)/shard_map/ppermute | solution.py:93
  79.4 44.2 %collective-permute-start.8 = (bf16[4,256,256]{2,1,0:T(8,128)(2,1)S(1)}, bf16[4,256,256]{2,1,0:T(8,128)(2,1)S(1)}, u32[]{:S(2)}, u32[]{:S(2)}) collective-permute-start(bf16[4,256,256]{2,1,0:T(8,128)(2,1)S(1)} %get-tuple-element.28), channel_id=1, source_target_pairs={{0,16},{8,24},{16,0},{24,8},{1,17},{9,25},{17,1},{25,9},{2,18},{10... | collective-permute-start | bytes 1572872 | tf_op jit(solution)/shard_map/ppermute | solution.py:93
  101.8 44.2 %collective-permute-start.6 = (bf16[4,256,256]{2,1,0:T(8,128)(2,1)S(1)}, bf16[4,256,256]{2,1,0:T(8,128)(2,1)S(1)}, u32[]{:S(2)}, u32[]{:S(2)}) collective-permute-start(bf16[4,256,256]{2,1,0:T(8,128)(2,1)S(1)} %get-tuple-element.25), channel_id=1, source_target_pairs={{0,16},{8,24},{16,0},{24,8},{1,17},{9,25},{17,1},{25,9},{2,18},{10... | collective-permute-start | bytes 1572872 | tf_op jit(solution)/shard_map/ppermute | solution.py:93
  101.8 45.1 %collective-permute-start = (f32[4,4]{1,0:T(4,128)S(1)}, f32[4,4]{1,0:T(4,128)S(1)}, u32[]{:S(2)}, u32[]{:S(2)}) collective-permute-start(f32[4,4]{1,0:T(4,128)S(1)} %bitcast.50), channel_id=1, source_target_pairs={{0,16},{8,24},{16,0},{24,8},{1,17},{9,25},{17,1},{25,9},{2,18},{10... | collective-permute-start | bytes 200 | tf_op jit(solution)/shard_map/ppermute | solution.py:93
  124.3 44.4 %collective-permute-start.12 = (bf16[4,256,256]{2,1,0:T(8,128)(2,1)}, bf16[4,256,256]{2,1,0:T(8,128)(2,1)}, u32[]{:S(2)}, u32[]{:S(2)}) collective-permute-start(bf16[4,256,256]{2,1,0:T(8,128)(2,1)} %get-tuple-element.34), channel_id=1, source_target_pairs={{0,16},{8,24},{16,0},{24,8},{1,17},{9,25},{17,1},{25,9},{2,18},{10... | collective-permute-start | bytes 1572872 | tf_op jit(solution)/shard_map/ppermute | solution.py:93
  146.8 34.0 %collective-permute-start.10 = (bf16[4,256,256]{2,1,0:T(8,128)(2,1)}, bf16[4,256,256]{2,1,0:T(8,128)(2,1)}, u32[]{:S(2)}, u32[]{:S(2)}) collective-permute-start(bf16[4,256,256]{2,1,0:T(8,128)(2,1)} %get-tuple-element.31), channel_id=1, source_target_pairs={{0,16},{8,24},{16,0},{24,8},{1,17},{9,25},{17,1},{25,9},{2,18},{10... | collective-permute-start | bytes 1572872 | tf_op jit(solution)/shard_map/ppermute | solution.py:93
  153.0 44.8 %collective-permute-start.3 = (bf16[4,4,64,256]{3,2,1,0:T(8,128)(2,1)S(1)}, bf16[4,4,64,256]{3,2,1,0:T(8,128)(2,1)S(1)}, u32[]{:S(2)}, u32[]{:S(2)}) collective-permute-start(bf16[4,4,64,256]{3,2,1,0:T(8,128)(2,1)S(1)} %bitcast.43), channel_id=1, source_target_pairs={{0,8},{8,0},{16,24},{24,16},{1,9},{9,1},{17,25},{25,17},{2,10},{10... | collective-permute-start | bytes 1572872 | tf_op jit(solution)/shard_map/ppermute | solution.py:97
  168.7 5.1 %copy-start.6 = (bf16[4,256,256]{2,1,0:T(8,128)(2,1)S(1)}, bf16[4,256,256]{2,1,0:T(8,128)(2,1)}, u32[]{:S(2)}) copy-start(bf16[4,256,256]{2,1,0:T(8,128)(2,1)} %copy-done.5) | copy-start | bytes 1572868
  173.8 67.1 %collective-permute-start.13 = (bf16[4,4,64,256]{3,2,1,0:T(8,128)(2,1)S(1)}, bf16[4,4,64,256]{3,2,1,0:T(8,128)(2,1)S(1)}, u32[]{:S(2)}, u32[]{:S(2)}) collective-permute-start(bf16[4,4,64,256]{3,2,1,0:T(8,128)(2,1)S(1)} %bitcast.41), channel_id=1, source_target_pairs={{0,8},{8,0},{16,24},{24,16},{1,9},{9,1},{17,25},{25,17},{2,10},{10... | collective-permute-start | bytes 1572872 | tf_op jit(solution)/shard_map/ppermute | solution.py:97
  178.8 31.0 %collective-permute-start.5 = (bf16[4,4,64,256]{3,2,1,0:T(8,128)(2,1)S(1)}, bf16[4,4,64,256]{3,2,1,0:T(8,128)(2,1)S(1)}, u32[]{:S(2)}, u32[]{:S(2)}) collective-permute-start(bf16[4,4,64,256]{3,2,1,0:T(8,128)(2,1)S(1)} %bitcast.44), channel_id=1, source_target_pairs={{0,8},{8,0},{16,24},{24,16},{1,9},{9,1},{17,25},{25,17},{2,10},{10... | collective-permute-start | bytes 1572872 | tf_op jit(solution)/shard_map/ppermute | solution.py:97
  180.8 5.1 %copy-start.4 = (bf16[4,256,256]{2,1,0:T(8,128)(2,1)S(1)}, bf16[4,256,256]{2,1,0:T(8,128)(2,1)}, u32[]{:S(2)}) copy-start(bf16[4,256,256]{2,1,0:T(8,128)(2,1)} %copy-done.3) | copy-start | bytes 1572868
  185.9 54.8 %collective-permute-start.11 = (bf16[4,4,64,256]{3,2,1,0:T(8,128)(2,1)S(1)}, bf16[4,4,64,256]{3,2,1,0:T(8,128)(2,1)S(1)}, u32[]{:S(2)}, u32[]{:S(2)}) collective-permute-start(bf16[4,4,64,256]{3,2,1,0:T(8,128)(2,1)S(1)} %bitcast.42), channel_id=1, source_target_pairs={{0,8},{8,0},{16,24},{24,16},{1,9},{9,1},{17,25},{25,17},{2,10},{10... | collective-permute-start | bytes 1572872 | tf_op jit(solution)/shard_map/ppermute | solution.py:97
  186.0 7.0 %copy-start.2 = (bf16[4,256,256]{2,1,0:T(8,128)(2,1)S(1)}, bf16[4,256,256]{2,1,0:T(8,128)(2,1)}, u32[]{:S(2)}) copy-start(bf16[4,256,256]{2,1,0:T(8,128)(2,1)} %copy-done.1) | copy-start | bytes 1572868
  190.9 41.4 %collective-permute-start.7 = (bf16[4,4,64,256]{3,2,1,0:T(8,128)(2,1)S(1)}, bf16[4,4,64,256]{3,2,1,0:T(8,128)(2,1)S(1)}, u32[]{:S(2)}, u32[]{:S(2)}) collective-permute-start(bf16[4,4,64,256]{3,2,1,0:T(8,128)(2,1)S(1)} %bitcast.45), channel_id=1, source_target_pairs={{0,8},{8,0},{16,24},{24,16},{1,9},{9,1},{17,25},{25,17},{2,10},{10... | collective-permute-start | bytes 1572872 | tf_op jit(solution)/shard_map/ppermute | solution.py:97
  197.9 42.6 %collective-permute-start.9 = (bf16[4,4,64,256]{3,2,1,0:T(8,128)(2,1)S(1)}, bf16[4,4,64,256]{3,2,1,0:T(8,128)(2,1)S(1)}, u32[]{:S(2)}, u32[]{:S(2)}) collective-permute-start(bf16[4,4,64,256]{3,2,1,0:T(8,128)(2,1)S(1)} %bitcast.46), channel_id=1, source_target_pairs={{0,8},{8,0},{16,24},{24,16},{1,9},{9,1},{17,25},{25,17},{2,10},{10... | collective-permute-start | bytes 1572872 | tf_op jit(solution)/shard_map/ppermute | solution.py:97
  240.8 1.7 copy-start.9
  (5 other events, 4.3 us)
Sparse Core Ops, SparseCore 0:
  39.1 55.5 all-gather.1

commit v2 on v1

v2 whole, which is shorter than its diff:
```python
import functools

import jax
import jax.numpy as jnp
from jax import lax
from jax.experimental import pallas as pl
from jax.experimental.pallas import tpu as pltpu
from jax.sharding import PartitionSpec as P


def block_kernel(hi, rows, narrow, order, sector, right_dims, mpo, psi, *refs):
    lefts, rights = refs[:hi], refs[hi : 2 * hi]
    keep, send = refs[2 * hi :]
    states = psi.shape[1]
    stacked = jnp.concatenate([left[0] for left in lefts], axis=0)
    parts = [
        jnp.dot(stacked, psi[0, p], preferred_element_type=jnp.float32) for p in range(states)
    ]
    total = None
    for i in range(hi):
        right = rights[i][0]
        if not narrow:
            r = right_dims[order[pl.program_id(0)]]
            inside = (lax.broadcasted_iota(jnp.int32, right.shape, 0) < r) & (
                lax.broadcasted_iota(jnp.int32, right.shape, 1) < r
            )
            right = jnp.where(inside, right, jnp.zeros_like(right))
        mixed = []
        for s in range(states):
            acc = None
            for p in range(states):
                piece = parts[p][i * rows : (i + 1) * rows] * mpo[i, s * states + p]
                acc = piece if acc is None else acc + piece
            mixed.append(acc.astype(jnp.bfloat16))
        mixed = jnp.concatenate(mixed, axis=0)
        product = lax.dot_general(
            mixed, right, (((1,), (1,)), ((), ())), preferred_element_type=jnp.float32
        )
        total = product if total is None else total + product
    own = keep.shape[2]
    for s in range(states):
        keep[0, s] = total[s * rows : s * rows + own].astype(keep.dtype)
        for j in range(send.shape[1]):
            at = s * rows + (j + 1) * own
            send[0, j, s] = total[at : at + own].astype(send.dtype)


def blocks_call(hi, lo, own_rows, narrow, order, sector, right_dims, mpo, psi, lefts, right, others):
    states, width = psi.shape[1], psi.shape[2]
    count = order.shape[0]
    across = width // 2 if narrow else width
    rows = lo * own_rows

    def by_block(k, order, sector, *_):
        return (order[k], 0, 0)

    def by_sector(k, order, sector, *_):
        return (sector[order[k]], 0, 0)

    grid_spec = pltpu.PrefetchScalarGridSpec(
        num_scalar_prefetch=4,
        grid=(count,),
        in_specs=[
            pl.BlockSpec((1, states, width, across), lambda *at: by_block(*at) + (0,)),
        ]
        + [pl.BlockSpec((1, rows, width), by_sector)] * hi
        + [pl.BlockSpec((1, across, across), by_block)]
        + [pl.BlockSpec((1, across, across), lambda k, *_: (k, 0, 0))] * (hi - 1),
        out_specs=[
            pl.BlockSpec((1, states, own_rows, across), lambda k, *_: (k, 0, 0, 0)),
            pl.BlockSpec((1, lo - 1, states, own_rows, across), lambda k, *_: (k, 0, 0, 0, 0)),
        ],
    )
    return pl.pallas_call(
        functools.partial(block_kernel, hi, rows, narrow),
        grid_spec=grid_spec,
        out_shape=[
            jax.ShapeDtypeStruct((count, states, own_rows, across), jnp.bfloat16),
            jax.ShapeDtypeStruct((count, lo - 1, states, own_rows, across), jnp.bfloat16),
        ],
        compiler_params=pltpu.CompilerParams(vmem_limit_bytes=48 * 2**20),
        cost_estimate=pl.CostEstimate(
            flops=count * 2 * hi * rows * states * across * (width + across),
            bytes_accessed=count * 5 * states * width * across,
            transcendentals=0,
        ),
    )(order, sector, right_dims, mpo, psi, *lefts, right, *others)


def add_kernel(terms, order, *refs):
    out = refs[-1]
    total = refs[0][0].astype(jnp.float32)
    for j in range(1, terms):
        total = total + refs[j][0].astype(jnp.float32)
    across = total.shape[-1]
    out[0, :, :, :across] = total.astype(out.dtype)
    if across < out.shape[-1]:
        out[0, :, :, across:] = jnp.zeros(out.shape[1:3] + (out.shape[-1] - across,), out.dtype)


def add_call(shape, order, terms, out):
    block = pl.BlockSpec((1,) + terms[0].shape[1:], lambda k, order: (k, 0, 0, 0))
    grid_spec = pltpu.PrefetchScalarGridSpec(
        num_scalar_prefetch=1,
        grid=(order.shape[0],),
        in_specs=[block] * len(terms) + ([] if out is None else [pl.BlockSpec(memory_space=pl.ANY)]),
        out_specs=pl.BlockSpec((1,) + shape[1:], lambda k, order: (order[k], 0, 0, 0)),
    )
    return pl.pallas_call(
        functools.partial(add_kernel, len(terms)),
        grid_spec=grid_spec,
        out_shape=jax.ShapeDtypeStruct(shape, jnp.bfloat16),
        input_output_aliases={} if out is None else {1 + len(terms): 0},
        compiler_params=pltpu.CompilerParams(vmem_limit_bytes=32 * 2**20),
        cost_estimate=pl.CostEstimate(
            flops=terms[0].size, bytes_accessed=6 * terms[0].size, transcendentals=0
        ),
    )(order, *terms, *([] if out is None else [out]))


def after(x, *others):
    return lax.optimization_barrier((x, others))[0]


def on_device(n_chan, psi, mpo, left_env, right_env, left_dims, right_dims, dest_owner, left_slot):
    blocks, states, width = psi.shape[:3]
    sectors = left_env.shape[1]
    half = width // 2
    hi = 2 if n_chan % 2 == 0 else 1
    lo = n_chan // hi
    own_rows = width // n_chan
    here = lax.axis_index("chan")
    h, l = here // lo, here % lo
    right = right_env[0]

    def over_hi(x, i):
        pairs = [(c, ((c // lo + i) % hi) * lo + c % lo) for c in range(n_chan)]
        return lax.ppermute(x, "chan", pairs)

    def over_lo(x, j):
        pairs = [(c, (c // lo) * lo + (c % lo + j) % lo) for c in range(n_chan)]
        return lax.ppermute(x, "chan", pairs)

    def to_partners(x):
        return [over_hi(x, i) for i in range(1, hi)]

    wide = right_dims > half
    n_wide = jnp.sum(wide.astype(jnp.int32))
    most_wide = lax.pmax(n_wide, "sec")
    ids = jnp.arange(blocks, dtype=jnp.int32)
    before = ids[None, :] < ids[:, None]
    ahead = jnp.sum((before & (wide[None, :] == wide[:, None])).astype(jnp.int32), axis=1)
    place = jnp.where(wide, ahead, n_wide + ahead)
    order = jnp.sum(jnp.where(place[None, :] == ids[:, None], ids[None, :], 0), axis=1)
    sector = dest_owner[:, 0] * sectors + left_slot

    step = max(blocks // 6, 1)

    def wide_piece(span):
        return jnp.take(right, order[span], axis=0, mode="clip")

    def narrow_piece(span):
        return jnp.take(right[:, :half, :half], order[span], axis=0, mode="clip")

    left_mask = (jnp.arange(width, dtype=jnp.int32)[None, :] < left_dims[:, None]).astype(jnp.bfloat16)
    left_kept = left_env[0] * (left_mask[:, :, None] * left_mask[:, None, :])
    left_kept = left_kept.reshape(sectors, hi, lo, own_rows, width)
    left_kept = jnp.take(left_kept, (l + jnp.arange(lo)) % lo, axis=2)

    def for_half(i):
        picked = lax.dynamic_index_in_dim(left_kept, (h + i) % hi, axis=1, keepdims=False)
        return picked.reshape(sectors, lo * own_rows, width)

    shards = [for_half(0)] + [over_hi(for_half(i), i) for i in range(1, hi)]
    mpos = [mpo[0]] + to_partners(mpo[0])
    mpo_all = jnp.stack(mpos).reshape(hi, states * states)
    lefts = []
    for shard in shards:
        if lefts:
            shard = after(shard, lefts[-1])
        else:
            shard = after(shard, most_wide)
        lefts.append(lax.all_gather(shard, "sec", axis=0, tiled=True))

    early = [slice(0, step), slice(step, 2 * step)]
    moved = [to_partners(wide_piece(span)) for span in early]

    def run(cap, order, moved, lefts, mpo_all):
        spans = [(slice(a, min(a + step, cap)), False) for a in range(0, cap, step)]
        rest = blocks - cap
        pieces = -(-rest // max(step + 1, 1))
        for q in range(pieces):
            a, b = cap + rest * q // pieces, cap + rest * (q + 1) // pieces
            spans.append((slice(a, b), True))
        moved = list(moved)
        keeps, sends = [], []

        def compute(m):
            span, narrow = spans[m]
            keep, send = blocks_call(
                hi, lo, own_rows, narrow, order[span], sector, right_dims, mpo_all,
                psi, lefts, right, moved[m],
            )
            keeps.append(keep)
            sends.append(send)

        for m in range(len(moved), len(spans)):
            span, narrow = spans[m]
            piece = narrow_piece(span) if narrow else wide_piece(span)
            if m - 3 >= 0:
                compute(m - 3)
                piece = after(piece, moved[m - 2], sends[m - 3])
            moved.append(to_partners(piece))
        for m in range(len(sends), len(spans)):
            compute(m)
        out = None
        for m, (span, narrow) in enumerate(spans):
            arrived = [over_lo(sends[m][:, j - 1], j) for j in range(1, lo)]
            terms = [after(keeps[m], sends[min(m + 2, len(spans) - 1)])] + arrived
            out = add_call((blocks, states, own_rows, width), order[span], terms, out)
        return out

    caps = sorted({max(2 * step, blocks * q // 12) for q in (7, 8, 9)} | {blocks})
    which = sum((most_wide > cap).astype(jnp.int32) for cap in caps[:-1])
    return lax.switch(
        which, [functools.partial(run, cap) for cap in caps], order, moved, lefts, mpo_all
    )


def solution(mesh):
    in_specs = (
        P("sec", None, None, None),
        P("chan", None, None),
        P("chan", "sec", None, None),
        P("chan", "sec", None, None),
        P("sec"),
        P("sec"),
        P("sec", None),
        P("sec"),
    )
    out_specs = P("sec", None, "chan", None)
    return jax.shard_map(
        functools.partial(on_device, mesh.shape["chan"]),
        mesh=mesh,
        in_specs=in_specs,
        out_specs=out_specs,
        check_vma=False,
    )
```

time: 251 us -> 224 us (0.89)
  waiting for transfers between devices: 178 us -> 104 us
  Pallas kernels: 29.7 us -> 47.9 us
  local copies, waits for them, and re-layouts: 9.21 us -> 19.6 us
  blocking collectives: 0 us -> 10.2 us
  starting transfers between devices: 14.5 us -> 19.3 us
    ppermute x8, waiting for transfers between devices: 136 us -> 90.5 us  [over_hi(): return lax.ppermute(x, 'chan', pairs)]
    ppermute x6, waiting for transfers between devices: 42 us -> 1.77 us  [over_lo(): return lax.ppermute(x, 'chan', pairs)]
    pallas_call x6 -> x12, Pallas kernels: 29.7 us -> 47.9 us  [the longest x6 34.2 us: blocks_call(): pl.pallas_call(functools.partial(block_kernel, hi, rows, narrow), grid_sp...]
    gather x0 -> x6, local copies, waits for them, and re-layouts: none -> 15.5 us  [the longest x4 11.5 us: wide_piece(): return jnp.take(right, order[span], axis=0, mode='clip')]
    all_gather x1 -> x2, waiting for transfers between devices: 0.02 us -> 12.1 us  [on_device(): lefts.append(lax.all_gather(shard, 'sec', axis=0, tiled=True))]
    pmax x0 -> x1, blocking collectives: none -> 10.2 us  [on_device(): most_wide = lax.pmax(n_wide, 'sec')]
    unnamed x28 -> x10, local copies, waits for them, and re-layouts: 5.94 us -> 0.03 us
    ppermute x6, starting transfers between devices: 4.55 us -> 7.75 us  [over_lo(): return lax.ppermute(x, 'chan', pairs)]
  transfers between devices with their start and end apart: 15 -> 16, of which waited for: 9 -> 7; matrix products, arithmetic and copies ran while one was open for 1% -> 7% of each run, Pallas kernels for 12% -> 21%
where the time goes in v2:
time: 224 us; the launch traced here: 223 us
  waiting for transfers between devices  104 us (46%)
  Pallas kernels  47.9 us (21%)
  local copies, waits for them, and re-layouts  19.6 us (9%)
  starting transfers between devices  19.3 us (9%)
  between operations  15.7 us (7%)
  blocking collectives  10.2 us (5%)
  other arithmetic  5.49 us (2%)
    ppermute x8, waiting for transfers between devices, over_hi(): return lax.ppermute(x, 'chan', pairs)  90.5 us
    pallas_call x6, Pallas kernels, blocks_call(): pl.pallas_call(functools.partial(block_kernel, hi, rows, narrow), grid_sp...  34.2 us
    pallas_call x6, Pallas kernels, add_call(): pl.pallas_call(functools.partial(add_kernel, len(terms)), grid_spec=grid_...  13.6 us
    all_gather x2, waiting for transfers between devices, on_device(): lefts.append(lax.all_gather(shard, 'sec', axis=0, tiled=True))  12.1 us
    gather x4, local copies, waits for them, and re-layouts, wide_piece(): return jnp.take(right, order[span], axis=0, mode='clip')  11.5 us
    ppermute x8, starting transfers between devices, over_hi(): return lax.ppermute(x, 'chan', pairs)  11.5 us
    pmax x1, blocking collectives, on_device(): most_wide = lax.pmax(n_wide, 'sec')  10.2 us
    ppermute x6, starting transfers between devices, over_lo(): return lax.ppermute(x, 'chan', pairs)  7.75 us
  transfers between devices with their start and end apart: 16, of which 7 were waited for; matrix products, arithmetic and copies ran while one was open for 7% of the time, Pallas kernels for 21%

profile of v2, /device:TPU:0, one launch (start us, length us, event | category | flops | bytes accessed | tf_op | source)
XLA Modules:
  0.0 222.8 jit_solution(4812093605764793638)
XLA Ops:
  12.7 10.2 %pmax.7 = s32[]{:T(128)} all-reduce(s32[]{:T(128)} %convert_reduce_fusion.1), channel_id=1, replica_groups=mesh['chan'=4,'sec'=8] {'sec'}, use_global_device_ids=true, to_apply=%region_1.2 | all-reduce | flops 1 | bytes 8 | tf_op jit(solution)/shard_map/pmax | solution.py:149
  23.0 2.7 %collective-permute-start.43 = (bf16[8,128,256]{2,1,0:T(8,128)(2,1)S(1)}, bf16[8,128,256]{2,1,0:T(8,128)(2,1)S(1)}, u32[]{:S(2)}, u32[]{:S(2)}) collective-permute-start(bf16[8,128,256]{2,1,0:T(8,128)(2,1)S(1)} %bitcast.65), channel_id=1, source_target_pairs={{0,16},{8,24},{16,0},{24,8},{1,17},{9,25},{17,1},{25,9},{2,18},{10... | collective-permute-start | bytes 1572872 | tf_op jit(solution)/shard_map/ppermute | solution.py:138
  25.7 21.7 %collective-permute-done.43 = bf16[8,128,256]{2,1,0:T(8,128)(2,1)S(1)} collective-permute-done((bf16[8,128,256]{2,1,0:T(8,128)(2,1)S(1)}, bf16[8,128,256]{2,1,0:T(8,128)(2,1)S(1)}, u32[]{:S(2)}, u32[]{:S(2)}) %collective-permute-start.43) | collective-permute-done | bytes 524320 | tf_op jit(solution)/shard_map/ppermute | solution.py:138
  47.3 12.1 %all-gather.3.cloned.1.call-done = bf16[64,128,256]{2,1,0:T(8,128)(2,1)} async-done(((bf16[8,128,256]{2,1,0:T(8,128)(2,1)}), bf16[64,128,256]{2,1,0:T(8,128)(2,1)}) %all-gather.3.cloned.1.call-update) | async-done | bytes 4194320 | tf_op jit(solution)/shard_map/all_gather | solution.py:183
  60.5 2.5 %gather_fusion.18 = bf16[4,256,256]{2,1,0:T(8,128)(2,1)S(1)} fusion(bf16[24,256,256]{2,1,0:T(8,128)(2,1)} %bitcast.57, s32[1024]{0:T(1024)S(1)} %pad_clamp_fusion.18), kind=kCustom, calls=%fused_computation.18 | custom fusion | bytes 1048592 | tf_op jit(solution)/shard_map/jit(_take)/gather | solution.py:160
  63.0 2.5 %collective-permute-start.44 = (bf16[4,256,256]{2,1,0:T(8,128)(2,1)S(1)}, bf16[4,256,256]{2,1,0:T(8,128)(2,1)S(1)}, u32[]{:S(2)}, u32[]{:S(2)}) collective-permute-start(bf16[4,256,256]{2,1,0:T(8,128)(2,1)S(1)} %gather_fusion.18), channel_id=1, source_target_pairs={{0,16},{8,24},{16,0},{24,8},{1,17},{9,25},{17,1},{25,9},{2,18},{10... | collective-permute-start | bytes 1572872 | tf_op jit(solution)/shard_map/ppermute | solution.py:138
  65.5 2.5 %gather_fusion.19 = bf16[4,256,256]{2,1,0:T(8,128)(2,1)S(1)} fusion(bf16[24,256,256]{2,1,0:T(8,128)(2,1)} %bitcast.58, s32[1024]{0:T(1024)S(1)} %pad_clamp_fusion.17), kind=kCustom, calls=%fused_computation.19 | custom fusion | bytes 1048592 | tf_op jit(solution)/shard_map/jit(_take)/gather | solution.py:160
  68.5 2.4 %collective-permute-start.42 = (f32[4,4]{1,0:T(4,128)S(1)}, f32[4,4]{1,0:T(4,128)S(1)}, u32[]{:S(2)}, u32[]{:S(2)}) collective-permute-start(f32[4,4]{1,0:T(4,128)S(1)} %bitcast.66), channel_id=1, source_target_pairs={{0,16},{8,24},{16,0},{24,8},{1,17},{9,25},{17,1},{25,9},{2,18},{10... | collective-permute-start | bytes 200 | tf_op jit(solution)/shard_map/ppermute | solution.py:138
  73.1 38.8 %collective-permute-done.42 = f32[4,4]{1,0:T(4,128)S(1)} collective-permute-done((f32[4,4]{1,0:T(4,128)S(1)}, f32[4,4]{1,0:T(4,128)S(1)}, u32[]{:S(2)}, u32[]{:S(2)}) %collective-permute-start.42) | collective-permute-done | bytes 96 | tf_op jit(solution)/shard_map/ppermute | solution.py:138
  112.1 103.9 %conditional.1 = (bf16[24,4,64,256]{3,2,1,0:T(8,128)(2,1)}) conditional(s32[]{:T(128)} %clamp.3, (s32[24]{0:T(128)S(1)}, bf16[24,256,256]{2,1,0:T(8,128)(2,1)}, s32[24]{0:T(128)S(1)}, s32[24]{0:T(128)S(1)}, f32[2,16]{1,0:T(2,128)S(1)}, /*index=5*/bf16[24,4,256,256]{3,2,1,0:T(8,128)(2,1)}, ...), branch_computations={%region_4.5_spmd, %region_5.6_spmd, %region_6.7_spmd, %region_7.8_... | conditional | flops 6444027904 | bytes 188236800 | solution.py:225
  112.3 3.3 %gather_fusion.6 = bf16[4,256,256]{2,1,0:T(8,128)(2,1)} fusion(bf16[24,256,256]{2,1,0:T(8,128)(2,1)} %get-tuple-element.131.refs_2_, s32[1024]{0:T(1024)S(1)} %pad_clamp_fusion.5), kind=kCustom, calls=%fused_computation.6 | custom fusion | bytes 1048592 | tf_op jit(solution)/shard_map/cond/branch_1_fun/jit(_take)/gather | solution.py:160
  115.6 3.3 %gather_fusion.5 = bf16[4,256,256]{2,1,0:T(8,128)(2,1)} fusion(bf16[24,256,256]{2,1,0:T(8,128)(2,1)} %get-tuple-element.131.refs_2_, s32[1024]{0:T(1024)S(1)} %get-tuple-element.235), kind=kCustom, calls=%fused_computation.5 | custom fusion | bytes 1048592 | tf_op jit(solution)/shard_map/cond/branch_1_fun/jit(_take)/gather | solution.py:160
  118.9 7.4 %branch_1_fun.12 = (bf16[4,4,64,256]{3,2,1,0:T(8,128)(2,1)S(1)}, bf16[4,1,4,64,256]{4,3,2,1,0:T(8,128)(2,1)}) custom-call(s32[4]{0:T(128)S(1)} %get-tuple-element.231.order, s32[24]{0:T(128)S(1)} %get-tuple-element.125.sector, s32[24]{0:T(128)S(1)} %get-tuple-element.126.right_dims, f32[2,16]{1,0:T(2,128)S(1)} %get-tuple-element.127.mpo, ...), custom_call_target="tpu_custom_call" | custom-call | flops 1073741824 | bytes 5242880 | tf_op jit(solution)/shard_map/cond/branch_1_fun/pallas_call | solution.py:74
  126.4 2.9 %collective-permute-start.10 = (bf16[4,256,256]{2,1,0:T(8,128)(2,1)}, bf16[4,256,256]{2,1,0:T(8,128)(2,1)S(1)}, u32[]{:S(2)}, u32[]{:S(2)}) collective-permute-start(bf16[4,256,256]{2,1,0:T(8,128)(2,1)} %gather_fusion.5), channel_id=1, source_target_pairs={{0,16},{8,24},{16,0},{24,8},{1,17},{9,25},{17,1},{25,9},{2,18},{10... | collective-permute-start | bytes 1572872 | tf_op jit(solution)/shard_map/cond/branch_1_fun/ppermute | solution.py:138
  130.2 5.6 %branch_1_fun.15 = (bf16[4,4,64,256]{3,2,1,0:T(8,128)(2,1)S(1)}, bf16[4,1,4,64,256]{4,3,2,1,0:T(8,128)(2,1)}) custom-call(s32[4]{0:T(128)S(1)} %get-tuple-element.228.order, s32[24]{0:T(128)S(1)} %get-tuple-element.125.sector, s32[24]{0:T(128)S(1)} %get-tuple-element.126.right_dims, f32[2,16]{1,0:T(2,128)S(1)} %get-tuple-element.127.mpo, ...), custom_call_target="tpu_custom_call" | custom-call | flops 1073741824 | bytes 5242880 | tf_op jit(solution)/shard_map/cond/branch_1_fun/pallas_call | solution.py:74
  140.7 13.3 %collective-permute-done.11.refs_3_ = bf16[4,256,256]{2,1,0:T(8,128)(2,1)S(1)} collective-permute-done((bf16[4,256,256]{2,1,0:T(8,128)(2,1)}, bf16[4,256,256]{2,1,0:T(8,128)(2,1)S(1)}, u32[]{:S(2)}, u32[]{:S(2)}) %collective-permute-start.11) | collective-permute-done | bytes 524320 | tf_op jit(solution)/shard_map/cond/branch_1_fun/ppermute | solution.py:138
  154.1 5.8 %branch_1_fun.13 = (bf16[4,4,64,256]{3,2,1,0:T(8,128)(2,1)S(1)}, bf16[4,1,4,64,256]{4,3,2,1,0:T(8,128)(2,1)}) custom-call(s32[4]{0:T(128)S(1)} %get-tuple-element.230.order, s32[24]{0:T(128)S(1)} %get-tuple-element.125.sector, s32[24]{0:T(128)S(1)} %get-tuple-element.126.right_dims, f32[2,16]{1,0:T(2,128)S(1)} %get-tuple-element.127.mpo, ...), custom_call_target="tpu_custom_call" | custom-call | flops 1073741824 | bytes 5242880 | tf_op jit(solution)/shard_map/cond/branch_1_fun/pallas_call | solution.py:74
  160.2 5.1 %collective-permute-done.10.refs_3_ = bf16[4,256,256]{2,1,0:T(8,128)(2,1)S(1)} collective-permute-done((bf16[4,256,256]{2,1,0:T(8,128)(2,1)}, bf16[4,256,256]{2,1,0:T(8,128)(2,1)S(1)}, u32[]{:S(2)}, u32[]{:S(2)}) %collective-permute-start.10) | collective-permute-done | bytes 524320 | tf_op jit(solution)/shard_map/cond/branch_1_fun/ppermute | solution.py:138
  165.3 5.6 %branch_1_fun.17 = (bf16[4,4,64,256]{3,2,1,0:T(8,128)(2,1)S(1)}, bf16[4,1,4,64,256]{4,3,2,1,0:T(8,128)(2,1)}) custom-call(s32[4]{0:T(128)S(1)} %get-tuple-element.232.order, s32[24]{0:T(128)S(1)} %get-tuple-element.125.sector, s32[24]{0:T(128)S(1)} %get-tuple-element.126.right_dims, f32[2,16]{1,0:T(2,128)S(1)} %get-tuple-element.127.mpo, ...), custom_call_target="tpu_custom_call" | custom-call | flops 1073741824 | bytes 5242880 | tf_op jit(solution)/shard_map/cond/branch_1_fun/pallas_call | solution.py:74
  173.6 5.5 %branch_1_fun.16 = (bf16[4,4,64,128]{3,2,1,0:T(8,128)(2,1)S(1)}, bf16[4,1,4,64,128]{4,3,2,1,0:T(8,128)(2,1)S(1)}) custom-call(s32[4]{0:T(128)S(1)} %get-tuple-element.229.order, s32[24]{0:T(128)S(1)} %get-tuple-element.125.sector, s32[24]{0:T(128)S(1)} %get-tuple-element.126.right_dims, f32[2,16]{1,0:T(2,128)S(1)} %get-tuple-element.127.mpo, ...), custom_call_target="tpu_custom_call" | custom-call | flops 402653184 | bytes 2621440 | tf_op jit(solution)/shard_map/cond/branch_1_fun/pallas_call | solution.py:74
  179.1 11.6 %collective-permute-done.12.refs_3_ = bf16[4,128,128]{2,1,0:T(8,128)(2,1)S(1)} collective-permute-done((bf16[4,128,128]{2,1,0:T(8,128)(2,1)}, bf16[4,128,128]{2,1,0:T(8,128)(2,1)S(1)}, u32[]{:S(2)}, u32[]{:S(2)}) %collective-permute-start.12) | collective-permute-done | bytes 131104 | tf_op jit(solution)/shard_map/cond/branch_1_fun/ppermute | solution.py:138
  190.7 5.3 %collective-permute-start.15 = (bf16[4,4,64,128]{3,2,1,0:T(8,128)(2,1)S(1)}, bf16[4,4,64,128]{3,2,1,0:T(8,128)(2,1)S(1)}, u32[]{:S(2)}, u32[]{:S(2)}) collective-permute-start(bf16[4,4,64,128]{3,2,1,0:T(8,128)(2,1)S(1)} %bitcast.50), channel_id=1, source_target_pairs={{0,8},{8,0},{16,24},{24,16},{1,9},{9,1},{17,25},{25,17},{2,10},{10... | collective-permute-start | bytes 786440 | tf_op jit(solution)/shard_map/cond/branch_1_fun/ppermute | solution.py:142
  196.0 4.4 %branch_1_fun.14 = (bf16[4,4,64,128]{3,2,1,0:T(8,128)(2,1)S(1)}, bf16[4,1,4,64,128]{4,3,2,1,0:T(8,128)(2,1)S(1)}) custom-call(s32[4]{0:T(128)S(1)} %get-tuple-element.233.order, s32[24]{0:T(128)S(1)} %get-tuple-element.125.sector, s32[24]{0:T(128)S(1)} %get-tuple-element.126.right_dims, f32[2,16]{1,0:T(2,128)S(1)} %get-tuple-element.127.mpo, ...), custom_call_target="tpu_custom_call" | custom-call | flops 402653184 | bytes 2621440 | tf_op jit(solution)/shard_map/cond/branch_1_fun/pallas_call | solution.py:74
  204.5 3.7 %branch_1_fun.20.refs_2_ = bf16[24,4,64,256]{3,2,1,0:T(8,128)(2,1)} custom-call(s32[4]{0:T(128)S(1)} %get-tuple-element.230.order, bf16[4,4,64,256]{3,2,1,0:T(8,128)(2,1)S(1)} %copy-done.3, bf16[4,4,64,256]{3,2,1,0:T(8,128)(2,1)} %collective-permute-done.17.refs_1_, bf16[24,4,64,256]{3,2,1,0:T(8,128)(2,1)} %branch_1_fun.19.refs_2_), custom_call_target="tpu_custom_call", output_to_operand_aliasing={{}: (3, {})} | custom-call | flops 262144 | bytes 1572864 | tf_op jit(solution)/shard_map/cond/branch_1_fun/pallas_call | solution.py:109
  (92 shorter events, 28.9 us)
Async XLA Ops:
  6.5 52.9 %all-gather.3.cloned.1.call-start = ((), (), s32[]{:S(2)}) async-start(), calls=%async_computation | async-start | bytes 4718592 | tf_op jit(solution)/shard_map/all_gather | solution.py:183
  11.7 47.8 %copy-start.24 = (s32[24]{0:T(128)S(1)}, s32[24]{0:T(128)}, u32[]{:S(2)}) copy-start(s32[24]{0:T(128)} %param.17) | copy-start | bytes 292
  11.8 56.7 %copy-start.27 = (f32[1,4,4]{2,1,0:T(4,128)S(1)}, f32[1,4,4]{2,1,0:T(4,128)}, u32[]{:S(2)}) copy-start(f32[1,4,4]{2,1,0:T(4,128)} %param.13) | copy-start | bytes 196
  11.9 61.2 %copy-start.28 = (s32[24]{0:T(128)S(1)}, s32[24]{0:T(128)}, u32[]{:S(2)}) copy-start(s32[24]{0:T(128)} %param.19) | copy-start | bytes 292
  11.9 61.2 %copy-start.29 = (s32[24,1]{0,1:T(1,128)S(1)}, s32[24,1]{0,1:T(1,128)}, u32[]{:S(2)}) copy-start(s32[24,1]{0,1:T(1,128)} %param.18) | copy-start | bytes 292
  22.9 89.1 %all-gather.5.cloned.1.call-start = ((), (), s32[]{:S(2)}) async-start(), calls=%async_computation.1 | async-start | bytes 4718592 | tf_op jit(solution)/shard_map/all_gather | solution.py:183
  23.0 24.3 %collective-permute-start.43 = (bf16[8,128,256]{2,1,0:T(8,128)(2,1)S(1)}, bf16[8,128,256]{2,1,0:T(8,128)(2,1)S(1)}, u32[]{:S(2)}, u32[]{:S(2)}) collective-permute-start(bf16[8,128,256]{2,1,0:T(8,128)(2,1)S(1)} %bitcast.65), channel_id=1, source_target_pairs={{0,16},{8,24},{16,0},{24,8},{1,17},{9,25},{17,1},{25,9},{2,18},{10... | collective-permute-start | bytes 1572872 | tf_op jit(solution)/shard_map/ppermute | solution.py:138
  63.0 49.0 %collective-permute-start.44 = (bf16[4,256,256]{2,1,0:T(8,128)(2,1)S(1)}, bf16[4,256,256]{2,1,0:T(8,128)(2,1)S(1)}, u32[]{:S(2)}, u32[]{:S(2)}) collective-permute-start(bf16[4,256,256]{2,1,0:T(8,128)(2,1)S(1)} %gather_fusion.18), channel_id=1, source_target_pairs={{0,16},{8,24},{16,0},{24,8},{1,17},{9,25},{17,1},{25,9},{2,18},{10... | collective-permute-start | bytes 1572872 | tf_op jit(solution)/shard_map/ppermute | solution.py:138
  67.9 44.1 %collective-permute-start.45 = (bf16[4,256,256]{2,1,0:T(8,128)(2,1)S(1)}, bf16[4,256,256]{2,1,0:T(8,128)(2,1)}, u32[]{:S(2)}, u32[]{:S(2)}) collective-permute-start(bf16[4,256,256]{2,1,0:T(8,128)(2,1)S(1)} %gather_fusion.19), channel_id=1, source_target_pairs={{0,16},{8,24},{16,0},{24,8},{1,17},{9,25},{17,1},{25,9},{2,18},{10... | collective-permute-start | bytes 1572872 | tf_op jit(solution)/shard_map/ppermute | solution.py:138
  68.5 43.4 %collective-permute-start.42 = (f32[4,4]{1,0:T(4,128)S(1)}, f32[4,4]{1,0:T(4,128)S(1)}, u32[]{:S(2)}, u32[]{:S(2)}) collective-permute-start(f32[4,4]{1,0:T(4,128)S(1)} %bitcast.66), channel_id=1, source_target_pairs={{0,16},{8,24},{16,0},{24,8},{1,17},{9,25},{17,1},{25,9},{2,18},{10... | collective-permute-start | bytes 200 | tf_op jit(solution)/shard_map/ppermute | solution.py:138
  115.6 38.5 %collective-permute-start.11 = (bf16[4,256,256]{2,1,0:T(8,128)(2,1)}, bf16[4,256,256]{2,1,0:T(8,128)(2,1)S(1)}, u32[]{:S(2)}, u32[]{:S(2)}) collective-permute-start(bf16[4,256,256]{2,1,0:T(8,128)(2,1)} %gather_fusion.6), channel_id=1, source_target_pairs={{0,16},{8,24},{16,0},{24,8},{1,17},{9,25},{17,1},{25,9},{2,18},{10... | collective-permute-start | bytes 1572872 | tf_op jit(solution)/shard_map/cond/branch_1_fun/ppermute | solution.py:138
  126.4 38.9 %collective-permute-start.10 = (bf16[4,256,256]{2,1,0:T(8,128)(2,1)}, bf16[4,256,256]{2,1,0:T(8,128)(2,1)S(1)}, u32[]{:S(2)}, u32[]{:S(2)}) collective-permute-start(bf16[4,256,256]{2,1,0:T(8,128)(2,1)} %gather_fusion.5), channel_id=1, source_target_pairs={{0,16},{8,24},{16,0},{24,8},{1,17},{9,25},{17,1},{25,9},{2,18},{10... | collective-permute-start | bytes 1572872 | tf_op jit(solution)/shard_map/cond/branch_1_fun/ppermute | solution.py:138
  129.3 71.2 %collective-permute-start.19 = (bf16[4,4,64,256]{3,2,1,0:T(8,128)(2,1)}, bf16[4,4,64,256]{3,2,1,0:T(8,128)(2,1)S(1)}, u32[]{:S(2)}, u32[]{:S(2)}) collective-permute-start(bf16[4,4,64,256]{3,2,1,0:T(8,128)(2,1)} %bitcast.11), channel_id=1, source_target_pairs={{0,8},{8,0},{16,24},{24,16},{1,9},{9,1},{17,25},{25,17},{2,10},{10... | collective-permute-start | bytes 1572872 | tf_op jit(solution)/shard_map/cond/branch_1_fun/ppermute | solution.py:142
  135.8 66.7 %collective-permute-start.18 = (bf16[4,4,64,256]{3,2,1,0:T(8,128)(2,1)}, bf16[4,4,64,256]{3,2,1,0:T(8,128)(2,1)S(1)}, u32[]{:S(2)}, u32[]{:S(2)}) collective-permute-start(bf16[4,4,64,256]{3,2,1,0:T(8,128)(2,1)} %bitcast.10), channel_id=1, source_target_pairs={{0,8},{8,0},{16,24},{24,16},{1,9},{9,1},{17,25},{25,17},{2,10},{10... | collective-permute-start | bytes 1572872 | tf_op jit(solution)/shard_map/cond/branch_1_fun/ppermute | solution.py:142
  140.7 24.6 %copy-start.5 = (bf16[64,128,256]{2,1,0:T(8,128)(2,1)S(1)}, bf16[64,128,256]{2,1,0:T(8,128)(2,1)}, u32[]{:S(2)}) copy-start(bf16[64,128,256]{2,1,0:T(8,128)(2,1)} %get-tuple-element.129.refs_0_) | copy-start | bytes 12582916 | tf_op jit(solution)/shard_map/cond
  140.7 24.6 %copy-start.11 = (bf16[64,128,256]{2,1,0:T(8,128)(2,1)S(1)}, bf16[64,128,256]{2,1,0:T(8,128)(2,1)}, u32[]{:S(2)}) copy-start(bf16[64,128,256]{2,1,0:T(8,128)(2,1)} %get-tuple-element.130.refs_1_) | copy-start | bytes 12582916 | tf_op jit(solution)/shard_map/cond
  140.7 24.6 %copy-start.16 = (bf16[24,256,256]{2,1,0:T(8,128)(2,1)S(1)}, bf16[24,256,256]{2,1,0:T(8,128)(2,1)}, u32[]{:S(2)}) copy-start(bf16[24,256,256]{2,1,0:T(8,128)(2,1)} %get-tuple-element.131.refs_2_) | copy-start | bytes 9437188 | tf_op jit(solution)/shard_map/cond
  154.1 19.1 %collective-permute-start.14 = (bf16[4,128,128]{2,1,0:T(8,128)(2,1)S(1)}, bf16[4,128,128]{2,1,0:T(8,128)(2,1)S(1)}, u32[]{:S(2)}, u32[]{:S(2)}) collective-permute-start(bf16[4,128,128]{2,1,0:T(8,128)(2,1)S(1)} %gather_fusion.7), channel_id=1, source_target_pairs={{0,16},{8,24},{16,0},{24,8},{1,17},{9,25},{17,1},{25,9},{2,18},{10... | collective-permute-start | bytes 393224 | tf_op jit(solution)/shard_map/cond/branch_1_fun/ppermute | solution.py:138
  159.8 44.7 %collective-permute-start.17 = (bf16[4,4,64,256]{3,2,1,0:T(8,128)(2,1)}, bf16[4,4,64,256]{3,2,1,0:T(8,128)(2,1)}, u32[]{:S(2)}, u32[]{:S(2)}) collective-permute-start(bf16[4,4,64,256]{3,2,1,0:T(8,128)(2,1)} %bitcast.9), channel_id=1, source_target_pairs={{0,8},{8,0},{16,24},{24,16},{1,9},{9,1},{17,25},{25,17},{2,10},{10... | collective-permute-start | bytes 1572872 | tf_op jit(solution)/shard_map/cond/branch_1_fun/ppermute | solution.py:142
  170.8 37.4 %collective-permute-start.16 = (bf16[4,4,64,256]{3,2,1,0:T(8,128)(2,1)}, bf16[4,4,64,256]{3,2,1,0:T(8,128)(2,1)S(1)}, u32[]{:S(2)}, u32[]{:S(2)}) collective-permute-start(bf16[4,4,64,256]{3,2,1,0:T(8,128)(2,1)} %bitcast.8), channel_id=1, source_target_pairs={{0,8},{8,0},{16,24},{24,16},{1,9},{9,1},{17,25},{25,17},{2,10},{10... | collective-permute-start | bytes 1572872 | tf_op jit(solution)/shard_map/cond/branch_1_fun/ppermute | solution.py:142
  173.2 22.8 %copy-start.17 = (bf16[24,256,256]{2,1,0:T(8,128)(2,1)S(1)}, bf16[24,256,256]{2,1,0:T(8,128)(2,1)}, u32[]{:S(2)}) copy-start(bf16[24,256,256]{2,1,0:T(8,128)(2,1)} %get-tuple-element.131.refs_2_) | copy-start | bytes 9437188 | tf_op jit(solution)/shard_map/cond
  173.2 17.5 %collective-permute-start.12 = (bf16[4,128,128]{2,1,0:T(8,128)(2,1)}, bf16[4,128,128]{2,1,0:T(8,128)(2,1)S(1)}, u32[]{:S(2)}, u32[]{:S(2)}) collective-permute-start(bf16[4,128,128]{2,1,0:T(8,128)(2,1)} %gather_fusion.4), channel_id=1, source_target_pairs={{0,16},{8,24},{16,0},{24,8},{1,17},{9,25},{17,1},{25,9},{2,18},{10... | collective-permute-start | bytes 393224 | tf_op jit(solution)/shard_map/cond/branch_1_fun/ppermute | solution.py:138
  190.7 19.5 %collective-permute-start.15 = (bf16[4,4,64,128]{3,2,1,0:T(8,128)(2,1)S(1)}, bf16[4,4,64,128]{3,2,1,0:T(8,128)(2,1)S(1)}, u32[]{:S(2)}, u32[]{:S(2)}) collective-permute-start(bf16[4,4,64,128]{3,2,1,0:T(8,128)(2,1)S(1)} %bitcast.50), channel_id=1, source_target_pairs={{0,8},{8,0},{16,24},{24,16},{1,9},{9,1},{17,25},{25,17},{2,10},{10... | collective-permute-start | bytes 786440 | tf_op jit(solution)/shard_map/cond/branch_1_fun/ppermute | solution.py:142
  200.4 13.5 %collective-permute-start.13 = (bf16[4,4,64,128]{3,2,1,0:T(8,128)(2,1)S(1)}, bf16[4,4,64,128]{3,2,1,0:T(8,128)(2,1)S(1)}, u32[]{:S(2)}, u32[]{:S(2)}) collective-permute-start(bf16[4,4,64,128]{3,2,1,0:T(8,128)(2,1)S(1)} %bitcast.51), channel_id=1, source_target_pairs={{0,8},{8,0},{16,24},{24,16},{1,9},{9,1},{17,25},{25,17},{2,10},{10... | collective-permute-start | bytes 786440 | tf_op jit(solution)/shard_map/cond/branch_1_fun/ppermute | solution.py:142
  (8 other events, 104.8 us)
Sparse Core Ops, SparseCore 0:
  23.0 36.3 all-gather.2
  61.3 36.7 all-gather.4

commit v3 on v1

v3 whole, which is shorter than its diff:
```python
import functools

import jax
import jax.numpy as jnp
from jax import lax
from jax.experimental import pallas as pl
from jax.experimental.pallas import tpu as pltpu
from jax.sharding import PartitionSpec as P

ANY = pl.BlockSpec(memory_space=pl.ANY)
SMEM = pl.BlockSpec(memory_space=pltpu.SMEM)


def after(x, *others):
    return lax.optimization_barrier((x, others))[0]


def left_kernel(hi, lo, here, dims, left, *outs):
    own = outs[0].shape[1] // lo
    h, l = here[0] // lo, here[0] % lo
    r = dims[pl.program_id(0)]
    for i in range(hi):
        for j in range(lo):
            start = pl.multiple_of((((h + i) % hi) * lo + (l + j) % lo) * own, own)
            piece = left[0, pl.ds(start, own), :]
            inside = (lax.broadcasted_iota(jnp.int32, piece.shape, 0) + start < r) & (
                lax.broadcasted_iota(jnp.int32, piece.shape, 1) < r
            )
            outs[i][0, j * own : (j + 1) * own] = jnp.where(inside, piece, jnp.zeros_like(piece))


def left_call(hi, lo, own_rows, here, dims, left):
    sectors, width = left.shape[:2]
    block = (1, lo * own_rows, width)
    return pl.pallas_call(
        functools.partial(left_kernel, hi, lo),
        grid_spec=pltpu.PrefetchScalarGridSpec(
            num_scalar_prefetch=2,
            grid=(sectors,),
            in_specs=[pl.BlockSpec((1, width, width), lambda s, *_: (s, 0, 0))],
            out_specs=[pl.BlockSpec(block, lambda s, *_: (s, 0, 0))] * hi,
        ),
        out_shape=[jax.ShapeDtypeStruct((sectors,) + block[1:], left.dtype)] * hi,
        compiler_params=pltpu.CompilerParams(vmem_limit_bytes=32 * 2**20),
        cost_estimate=pl.CostEstimate(flops=left.size, bytes_accessed=4 * left.size, transcendentals=0),
    )(here, dims, left)


def copy_pieces(order, right, pieces, spans, sems):
    copies = []
    for piece, span in zip(pieces, spans):
        across = piece.shape[-1]
        for n, at in enumerate(range(span.start, span.stop)):
            source = right.at[order[at]]
            if across < right.shape[-1]:
                source = right.at[order[at], pl.ds(0, across), pl.ds(0, across)]
            copies.append(pltpu.make_async_copy(source, piece.at[n], sems.at[len(copies)]))
    for copy in copies:
        copy.start()
    for copy in copies:
        copy.wait()


def plan_kernel(spans, dims, right, order, count, *refs):
    pieces, sems = refs[:-1], refs[-1]
    blocks, half = dims.shape[0], right.shape[-1] // 2

    def place(keep_wide):
        def body(k, at):
            mine = (dims[k] > half) == keep_wide

            @pl.when(mine)
            def _():
                order[at] = k

            return at + mine.astype(jnp.int32)

        return body

    wide = lax.fori_loop(0, blocks, place(True), jnp.int32(0))
    count[0] = wide
    lax.fori_loop(0, blocks, place(False), wide)
    copy_pieces(order, right, pieces, spans, sems)


def plan_call(spans, dims, right):
    width = right.shape[-1]
    total = sum(span.stop - span.start for span in spans)
    return pl.pallas_call(
        functools.partial(plan_kernel, spans),
        in_specs=[SMEM, ANY],
        out_specs=[SMEM, SMEM] + [ANY] * len(spans),
        out_shape=[jax.ShapeDtypeStruct(dims.shape, jnp.int32), jax.ShapeDtypeStruct((1,), jnp.int32)]
        + [jax.ShapeDtypeStruct((s.stop - s.start, width, width), right.dtype) for s in spans],
        scratch_shapes=[pltpu.SemaphoreType.DMA((total,))],
        cost_estimate=pl.CostEstimate(flops=0, bytes_accessed=4 * total * width * width, transcendentals=0),
    )(dims, right)


def pack_kernel(spans, order, right, *refs):
    copy_pieces(order, right, refs[:-1], spans, refs[-1])


def pack_call(spans, widths, order, right):
    total = sum(span.stop - span.start for span in spans)
    shapes = [jax.ShapeDtypeStruct((s.stop - s.start, w, w), right.dtype) for s, w in zip(spans, widths)]
    return pl.pallas_call(
        functools.partial(pack_kernel, spans),
        in_specs=[SMEM, ANY],
        out_specs=[ANY] * len(spans),
        out_shape=shapes,
        scratch_shapes=[pltpu.SemaphoreType.DMA((total,))],
        cost_estimate=pl.CostEstimate(
            flops=0, bytes_accessed=4 * sum(s.size for s in shapes), transcendentals=0
        ),
    )(order, right)


def pick_kernel(hi, order, near, row, *refs):
    sources, (*outs, sems) = refs[: 2 * hi], refs[2 * hi :]
    blocks = order.shape[0]

    def start(n, _):
        k = order[n]
        for i in range(hi):
            for far in range(2):

                @pl.when(near[k] == 1 - far)
                def _():
                    pltpu.make_async_copy(
                        sources[2 * i + far].at[row[k]], outs[i].at[n], sems.at[i, n]
                    ).start()

        return 0

    def finish(n, _):
        for i in range(hi):
            pltpu.make_async_copy(sources[2 * i].at[0], outs[i].at[n], sems.at[i, n]).wait()
        return 0

    lax.fori_loop(0, blocks, start, 0)
    lax.fori_loop(0, blocks, finish, 0)


def pick_call(hi, order, near, row, sources):
    blocks = order.shape[0]
    shape = (blocks,) + sources[0].shape[1:]
    return pl.pallas_call(
        functools.partial(pick_kernel, hi),
        in_specs=[SMEM] * 3 + [ANY] * (2 * hi),
        out_specs=[ANY] * hi,
        out_shape=[jax.ShapeDtypeStruct(shape, sources[0].dtype)] * hi,
        scratch_shapes=[pltpu.SemaphoreType.DMA((hi, blocks))],
        cost_estimate=pl.CostEstimate(
            flops=0, bytes_accessed=4 * hi * blocks * shape[1] * shape[2], transcendentals=0
        ),
    )(order, near, row, *sources)


def block_kernel(hi, rows, narrow, first, order, right_dims, mpo, psi, *refs):
    lefts, rights = refs[:hi], refs[hi : 2 * hi]
    keep, send = refs[2 * hi :]
    states = psi.shape[1]
    stacked = jnp.concatenate([left[0] for left in lefts], axis=0)
    parts = [
        jnp.dot(stacked, psi[0, p], preferred_element_type=jnp.float32) for p in range(states)
    ]
    total = None
    for i in range(hi):
        right = rights[i][0]
        if not narrow:
            r = right_dims[order[pl.program_id(0) + first]]
            inside = (lax.broadcasted_iota(jnp.int32, right.shape, 0) < r) & (
                lax.broadcasted_iota(jnp.int32, right.shape, 1) < r
            )
            right = jnp.where(inside, right, jnp.zeros_like(right))
        mixed = []
        for s in range(states):
            acc = None
            for p in range(states):
                piece = parts[p][i * rows : (i + 1) * rows] * mpo[i, s * states + p]
                acc = piece if acc is None else acc + piece
            mixed.append(acc.astype(jnp.bfloat16))
        mixed = jnp.concatenate(mixed, axis=0)
        product = lax.dot_general(
            mixed, right, (((1,), (1,)), ((), ())), preferred_element_type=jnp.float32
        )
        total = product if total is None else total + product
    own = keep.shape[2]
    for s in range(states):
        keep[0, s] = total[s * rows : s * rows + own].astype(keep.dtype)
        for j in range(send.shape[0]):
            at = s * rows + (j + 1) * own
            send[j, 0, s] = total[at : at + own].astype(send.dtype)


def blocks_call(hi, lo, own_rows, narrow, span, order, right_dims, mpo, psi, lefts, right, others):
    states, width = psi.shape[1], psi.shape[2]
    first, count = span.start, span.stop - span.start
    across = width // 2 if narrow else width
    rows = lo * own_rows

    def by_block(k, order, *_):
        return (order[k + first], 0, 0)

    grid_spec = pltpu.PrefetchScalarGridSpec(
        num_scalar_prefetch=3,
        grid=(count,),
        in_specs=[
            pl.BlockSpec((1, states, width, across), lambda *at: by_block(*at) + (0,)),
        ]
        + [pl.BlockSpec((1, rows, width), lambda k, *_: (k + first, 0, 0))] * hi
        + [pl.BlockSpec((1, across, across), by_block)]
        + [pl.BlockSpec((1, across, across), lambda k, *_: (k, 0, 0))] * (hi - 1),
        out_specs=[
            pl.BlockSpec((1, states, own_rows, across), lambda k, *_: (k, 0, 0, 0)),
            pl.BlockSpec((lo - 1, 1, states, own_rows, across), lambda k, *_: (0, k, 0, 0, 0)),
        ],
    )
    return pl.pallas_call(
        functools.partial(block_kernel, hi, rows, narrow, first),
        grid_spec=grid_spec,
        out_shape=[
            jax.ShapeDtypeStruct((count, states, own_rows, across), jnp.bfloat16),
            jax.ShapeDtypeStruct((lo - 1, count, states, own_rows, across), jnp.bfloat16),
        ],
        compiler_params=pltpu.CompilerParams(vmem_limit_bytes=40 * 2**20),
        cost_estimate=pl.CostEstimate(
            flops=count * 2 * hi * rows * states * across * (width + across),
            bytes_accessed=count * 5 * states * width * across,
            transcendentals=0,
        ),
    )(order, right_dims, mpo, psi, *lefts, right, *others)


def add_kernel(terms, span, order, *refs):
    out, total, sems = refs[-3:]
    across = refs[0].shape[-1]
    copies = []
    for k in range(span.stop - span.start):
        acc = refs[0][k].astype(jnp.float32)
        for j in range(1, terms):
            acc = acc + refs[j][k].astype(jnp.float32)
        total[k, :, :, :across] = acc.astype(total.dtype)
        if across < total.shape[-1]:
            total[k, :, :, across:] = jnp.zeros(acc.shape[:-1] + (total.shape[-1] - across,), total.dtype)
        copy = pltpu.make_async_copy(total.at[k], out.at[order[k + span.start]], sems.at[k])
        copy.start()
        copies.append(copy)
    for copy in copies:
        copy.wait()


def add_call(shape, span, order, terms, out):
    count = span.stop - span.start
    return pl.pallas_call(
        functools.partial(add_kernel, len(terms), span),
        in_specs=[SMEM]
        + [pl.BlockSpec(memory_space=pltpu.VMEM)] * len(terms)
        + ([] if out is None else [ANY]),
        out_specs=ANY,
        out_shape=jax.ShapeDtypeStruct(shape, jnp.bfloat16),
        scratch_shapes=[
            pltpu.VMEM((count,) + shape[1:], jnp.bfloat16),
            pltpu.SemaphoreType.DMA((count,)),
        ],
        input_output_aliases={} if out is None else {1 + len(terms): 0},
        compiler_params=pltpu.CompilerParams(vmem_limit_bytes=24 * 2**20),
        cost_estimate=pl.CostEstimate(
            flops=terms[0].size, bytes_accessed=6 * terms[0].size, transcendentals=0
        ),
    )(order, *terms, *([] if out is None else [out]))


def on_device(n_chan, n_sec, psi, mpo, left_env, right_env, left_dims, right_dims, dest_owner, left_slot):
    blocks, states, width = psi.shape[:3]
    sectors = left_env.shape[1]
    half = width // 2
    hi = 2 if n_chan % 2 == 0 else 1
    lo = n_chan // hi
    own_rows = width // n_chan
    here, me = lax.axis_index("chan"), lax.axis_index("sec")
    right = right_env[0]
    step = max(blocks // 6, 1)

    def over_hi(x, i):
        pairs = [(c, ((c // lo + i) % hi) * lo + c % lo) for c in range(n_chan)]
        return lax.ppermute(x, "chan", pairs)

    def over_lo(x, j):
        pairs = [(c, (c // lo) * lo + (c % lo + j) % lo) for c in range(n_chan)]
        return lax.ppermute(x, "chan", pairs)

    def over_bit(x, bit):
        return lax.ppermute(x, "sec", [(i, i ^ bit) for i in range(n_sec)])

    def to_partners(x):
        return [over_hi(x, i) for i in range(1, hi)]

    shards = left_call(hi, lo, own_rows, here[None], left_dims, left_env[0])
    early = [slice(m * step, (m + 1) * step) for m in range(3)]
    order, n_wide, *pieces = plan_call(early, right_dims, right)

    bits = [1 << b for b in range(1, n_sec.bit_length() - 1)]
    cut = sectors // 2

    def swap(i):
        if i == 0:
            return [shards[0][:cut], shards[0][cut:]]
        return [over_hi(shards[i][:cut], i), over_hi(shards[i][cut:], i)]

    def spread(parts):
        first, second = parts
        for bit, other in zip(bits, bits[::-1]):
            first = jnp.concatenate([first, over_bit(first, bit)])
            second = jnp.concatenate([second, over_bit(second, other)])
        near = jnp.concatenate([first, second])
        return [near, over_bit(near, 1)]

    gap = dest_owner[:, 0] ^ me
    up = sum(((gap // bit) % 2) << t for t, bit in enumerate(bits))
    down = sum(((gap // bit) % 2) << t for t, bit in enumerate(bits[::-1]))
    near = 1 - gap % 2
    row = jnp.where(
        left_slot < cut,
        up * cut + left_slot,
        (n_sec // 2) * cut + down * (sectors - cut) + left_slot - cut,
    )

    swapped = [swap(i) for i in range(hi)]
    mpo_all = jnp.stack([mpo[0]] + to_partners(mpo[0])).reshape(hi, states * states)
    sources = []
    for parts in swapped:
        sources += spread(parts)
    moved = [to_partners(after(pieces[0], swapped[-1][0]))]
    moved.append(to_partners(after(pieces[1], swapped[-1][1])))
    most_wide = lax.pmax(after(n_wide, moved[0]), "sec")[0]
    lefts = pick_call(hi, order, near, row, sources)

    def compute(span, narrow, order, lefts, mpo_all, others):
        return blocks_call(
            hi, lo, own_rows, narrow, span, order, right_dims, mpo_all, psi, lefts, right, others
        )

    def exchange(send):
        return [over_lo(send[j - 1], j) for j in range(1, lo)]

    keep, send = compute(early[0], False, order, lefts, mpo_all, moved[0])
    terms = [keep] + exchange(send)

    def run(cap, order, moved, third, lefts, mpo_all, terms):
        spans = [(slice(a, min(a + step, cap)), False) for a in range(0, cap, step)]
        rest = blocks - cap
        count = -(-rest // (step + 1))
        for q in range(count):
            a, b = cap + rest * q // count, cap + rest * (q + 1) // count
            spans.append((slice(a, b), True))
        total = len(spans)
        moved = list(moved)
        moved.append(to_partners(third))
        later = spans[3:]
        pieces = [third] * 3
        pieces += pack_call(
            [s for s, _ in later], [half if n else width for _, n in later], order, right
        )
        shape = (blocks, states, own_rows, width)
        terms = [terms]
        out = add_call(shape, spans[0][0], order, terms[0], None)
        added = 1
        for m in range(1, total):
            while added < m - 2:
                out = add_call(shape, spans[added][0], order, terms[added], out)
                added += 1
            mpo_now, out = lax.optimization_barrier((mpo_all, out))
            if m + 2 < total:
                waits = (moved[m], terms[m - 1][0]) if m > 1 else ()
                moved.append(to_partners(after(pieces[m + 2], waits)))
            keep, send = compute(*spans[m], order, lefts, mpo_now, moved[m])
            terms.append([keep] + exchange(send))
        for m in range(added, total):
            out = add_call(shape, spans[m][0], order, terms[m], out)
        return out

    caps = sorted({max(3 * step, blocks * q // 12) for q in (7, 8, 9)} | {blocks})
    which = sum((most_wide > cap).astype(jnp.int32) for cap in caps[:-1])
    return lax.switch(
        which,
        [functools.partial(run, cap) for cap in caps],
        order, moved, pieces[2], lefts, mpo_all, terms,
    )


def solution(mesh):
    in_specs = (
        P("sec", None, None, None),
        P("chan", None, None),
        P("chan", "sec", None, None),
        P("chan", "sec", None, None),
        P("sec"),
        P("sec"),
        P("sec", None),
        P("sec"),
    )
    out_specs = P("sec", None, "chan", None)
    return jax.shard_map(
        functools.partial(on_device, mesh.shape["chan"], mesh.shape["sec"]),
        mesh=mesh,
        in_specs=in_specs,
        out_specs=out_specs,
        check_vma=False,
    )
```

time: 251 us -> 277 us (1.10)
  Pallas kernels: 29.7 us -> 123 us
  waiting for transfers between devices: 178 us -> 98.6 us
  starting transfers between devices: 14.5 us -> 32.7 us
  between operations: 13.7 us -> 2.27 us
  blocking collectives: 0 us -> 7 us
  other arithmetic: 5.1 us -> 0.75 us
  local copies, waits for them, and re-layouts: 9.21 us -> 12.1 us
    pallas_call x6 -> x18, Pallas kernels: 29.7 us -> 123 us  [the longest x1 49.9 us: pick_call(): pl.pallas_call(functools.partial(pick_kernel, hi), in_specs=[SMEM] * 3 +...]
    ppermute x8 -> x10, waiting for transfers between devices: 136 us -> 67.2 us  [over_hi(): return lax.ppermute(x, 'chan', pairs)]
    ppermute x6 -> x7, waiting for transfers between devices: 42 us -> 10.7 us  [over_lo(): return lax.ppermute(x, 'chan', pairs)]
    ppermute x0 -> x10, waiting for transfers between devices: none -> 20.7 us  [over_bit(): return lax.ppermute(x, 'sec', [(i, i ^ bit) for i in range(n_sec)])]
    ppermute x0 -> x10, starting transfers between devices: none -> 11.1 us  [over_bit(): return lax.ppermute(x, 'sec', [(i, i ^ bit) for i in range(n_sec)])]
    pmax x0 -> x1, blocking collectives: none -> 7 us  [on_device(): most_wide = lax.pmax(after(n_wide, moved[0]), 'sec')[0]]
    ppermute x8 -> x10, starting transfers between devices: 9.96 us -> 15.5 us  [over_hi(): return lax.ppermute(x, 'chan', pairs)]
    unnamed x28 -> x23, local copies, waits for them, and re-layouts: 5.94 us -> 8.57 us
  transfers between devices with their start and end apart: 15 -> 27, of which waited for: 9 -> 11; matrix products, arithmetic and copies ran while one was open for 1% -> 3% of each run, Pallas kernels for 12% -> 44%
where the time goes in v3:
time: 277 us
  Pallas kernels  123 us (44%)
  waiting for transfers between devices  98.6 us (36%)
  starting transfers between devices  32.7 us (12%)
  local copies, waits for them, and re-layouts  12.1 us (4%)
  blocking collectives  7 us (3%)
    ppermute x10, waiting for transfers between devices, over_hi(): return lax.ppermute(x, 'chan', pairs)  67.2 us
    pallas_call x1, Pallas kernels, pick_call(): pl.pallas_call(functools.partial(pick_kernel, hi), in_specs=[SMEM] * 3 +...  49.9 us
    pallas_call x1, Pallas kernels, pack_call(): pl.pallas_call(functools.partial(pack_kernel, spans), in_specs=[SMEM, ANY...  31.5 us
    pallas_call x7, Pallas kernels, blocks_call(): pl.pallas_call(functools.partial(block_kernel, hi, rows, narrow, first),...  27.3 us
    ppermute x10, waiting for transfers between devices, over_bit(): return lax.ppermute(x, 'sec', [(i, i ^ bit) for i in range(n_sec)])  20.7 us
    ppermute x10, starting transfers between devices, over_hi(): return lax.ppermute(x, 'chan', pairs)  15.5 us
    ppermute x10, starting transfers between devices, over_bit(): return lax.ppermute(x, 'sec', [(i, i ^ bit) for i in range(n_sec)])  11.1 us
    ppermute x7, waiting for transfers between devices, over_lo(): return lax.ppermute(x, 'chan', pairs)  10.7 us
  transfers between devices with their start and end apart: 27, of which 11 were waited for; matrix products, arithmetic and copies ran while one was open for 3% of the time, Pallas kernels for 44%

profile of v3, /device:TPU:0, one launch (start us, length us, event | category | flops | bytes accessed | tf_op | source)
XLA Modules:
  0.0 276.6 jit_solution(7736580709520201897)
XLA Ops:
  3.9 2.9 %collective-permute-start.41 = (bf16[4,128,256]{2,1,0:T(8,128)(2,1)S(1)}, bf16[4,128,256]{2,1,0:T(8,128)(2,1)S(1)}, u32[]{:S(2)}, u32[]{:S(2)}) collective-permute-start(bf16[4,128,256]{2,1,0:T(8,128)(2,1)S(1)} %get-tuple-element.281), channel_id=1, source_target_pairs={{0,2},{1,3},{2,0},{3,1},{4,6},{5,7},{6,4},{7,5},{8,10},{9,11},{10,... | collective-permute-start | bytes 786440 | tf_op jit(solution)/shard_map/ppermute | solution.py:295
  6.8 2.7 collective-permute-start.48
  15.0 13.0 %collective-permute-done.48 = bf16[4,128,256]{2,1,0:T(8,128)(2,1)S(1)} collective-permute-done((bf16[4,128,256]{2,1,0:T(8,128)(2,1)S(1)}, bf16[4,128,256]{2,1,0:T(8,128)(2,1)S(1)}, u32[]{:S(2)}, u32[]{:S(2)}) %collective-permute-start.48) | collective-permute-done | bytes 262176 | tf_op jit(solution)/shard_map/ppermute | solution.py:288
  36.0 14.1 %collective-permute-done.46 = bf16[4,128,256]{2,1,0:T(8,128)(2,1)S(1)} collective-permute-done((bf16[4,128,256]{2,1,0:T(8,128)(2,1)S(1)}, bf16[4,128,256]{2,1,0:T(8,128)(2,1)S(1)}, u32[]{:S(2)}, u32[]{:S(2)}) %collective-permute-start.46) | collective-permute-done | bytes 262176 | tf_op jit(solution)/shard_map/ppermute | solution.py:295
  54.5 4.8 %collective-permute-done.47 = bf16[8,128,256]{2,1,0:T(8,128)(2,1)S(1)} collective-permute-done((bf16[8,128,256]{2,1,0:T(8,128)(2,1)S(1)}, bf16[8,128,256]{2,1,0:T(8,128)(2,1)S(1)}, u32[]{:S(2)}, u32[]{:S(2)}) %collective-permute-start.47) | collective-permute-done | bytes 524320 | tf_op jit(solution)/shard_map/ppermute | solution.py:295
  62.5 2.9 %shard_map.86 = (s32[24]{0:T(128)S(1)}, s32[1]{0:T(128)}, bf16[4,256,256]{2,1,0:T(8,128)(2,1)}, bf16[4,256,256]{2,1,0:T(8,128)(2,1)}, bf16[4,256,256]{2,1,0:T(8,128)(2,1)}) custom-call(s32[24]{0:T(128)S(1)} %copy-done.22, bf16[24,256,256]{2,1,0:T(8,128)(2,1)S(1)} %bitcast.85), custom_call_target="tpu_custom_call" | custom-call | bytes 3145728 | tf_op jit(solution)/shard_map/pallas_call | solution.py:89
  65.5 2.9 %collective-permute-start.40 = (f32[4,4]{1,0:T(4,128)S(1)}, f32[4,4]{1,0:T(4,128)S(1)}, u32[]{:S(2)}, u32[]{:S(2)}) collective-permute-start(f32[4,4]{1,0:T(4,128)S(1)} %bitcast.86), channel_id=1, source_target_pairs={{0,16},{8,24},{16,0},{24,8},{1,17},{9,25},{17,1},{25,9},{2,18},{10... | collective-permute-start | bytes 200 | tf_op jit(solution)/shard_map/ppermute | solution.py:288
  69.1 23.2 %collective-permute-done.40 = f32[4,4]{1,0:T(4,128)S(1)} collective-permute-done((f32[4,4]{1,0:T(4,128)S(1)}, f32[4,4]{1,0:T(4,128)S(1)}, u32[]{:S(2)}, u32[]{:S(2)}) %collective-permute-start.40) | collective-permute-done | bytes 96 | tf_op jit(solution)/shard_map/ppermute | solution.py:288
  92.5 49.9 %shard_map.88 = (bf16[24,128,256]{2,1,0:T(8,128)(2,1)S(1)}, bf16[24,128,256]{2,1,0:T(8,128)(2,1)}) custom-call(s32[24]{0:T(128)S(1)} %get-tuple-element.267.order, s32[24]{0:T(128)} %get-tuple-element.283.near, s32[24]{0:T(128)} %get-tuple-element.282.row, bf16[32,128,256]{2,1,0:T(8,128)(2,1)} %constant_dynamic-update-slice_fusion.refs_0_, ...), custom_call_target="tpu_custom_call" | custom-call | bytes 6291456 | tf_op jit(solution)/shard_map/pallas_call | solution.py:148
  142.3 5.6 %shard_map.89 = (bf16[4,4,64,256]{3,2,1,0:T(8,128)(2,1)}, bf16[1,4,4,64,256]{4,3,2,1,0:T(8,128)(2,1)S(1)}) custom-call(s32[24]{0:T(128)S(1)} %get-tuple-element.267.order, s32[24]{0:T(128)S(1)} %copy-done.22, f32[2,16]{1,0:T(2,128)S(1)} %pad_maximum_fusion.4.mpo, bf16[24,4,256,256]{3,2,1,0:T(8,128)(2,1)} %psi.1, ...), custom_call_target="tpu_custom_call" | custom-call | flops 1073741824 | bytes 5242880 | tf_op jit(solution)/shard_map/pallas_call | solution.py:220
  149.7 7.0 %pmax.7 = s32[1]{0:T(128)} all-reduce(s32[1]{0:T(128)} %get-tuple-element.266), channel_id=1, replica_groups=mesh['chan'=4,'sec'=8] {'sec'}, use_global_device_ids=true, to_apply=%region_0.1 | all-reduce | flops 1 | bytes 8 | tf_op jit(solution)/shard_map/pmax | solution.py:337
  158.7 2.9 %collective-permute-done.52 = bf16[4,4,64,256]{3,2,1,0:T(8,128)(2,1)S(1)} collective-permute-done((bf16[4,4,64,256]{3,2,1,0:T(8,128)(2,1)S(1)}, bf16[4,4,64,256]{3,2,1,0:T(8,128)(2,1)S(1)}, u32[]{:S(2)}, u32[]{:S(2)}) %collective-permute-start.52) | collective-permute-done | bytes 524320 | tf_op jit(solution)/shard_map/ppermute | solution.py:292
  161.6 114.8 %conditional.1 = (bf16[24,4,64,256]{3,2,1,0:T(8,128)(2,1)}) conditional(s32[]{:T(128)} %bitcast.24, (s32[24]{0:T(128)S(1)}, bf16[4,4,64,256]{3,2,1,0:T(8,128)(2,1)}, bf16[4,4,64,256]{3,2,1,0:T(8,128)(2,1)S(1)}, f32[2,16]{1,0:T(2,128)S(1)}, bf16[4,256,256]{2,1,0:T(8,128)(2,1)}, /*index=5*/s32[24]{0:T(128)S(1)}, ...), branch_computations={%region_1.2_spmd, %region_2.3_spmd, %region_3.4_spmd, %region_4.5_... | conditional | flops 5370281984 | bytes 172753568 | solution.py:386
  162.4 2.6 collective-permute-start.20
  165.0 31.5 %branch_2_fun.15 = (bf16[4,256,256]{2,1,0:T(8,128)(2,1)}, bf16[2,256,256]{2,1,0:T(8,128)(2,1)}, bf16[3,128,128]{2,1,0:T(8,128)(2,1)}, bf16[3,128,128]{2,1,0:T(8,128)(2,1)}) custom-call(s32[24]{0:T(128)S(1)} %get-tuple-element.170.order, bf16[24,256,256]{2,1,0:T(8,128)(2,1)} %get-tuple-element.181.right.refs_2_), custom_call_target="tpu_custom_call" | custom-call | bytes 1966080 | tf_op jit(solution)/shard_map/cond/branch_2_fun/pallas_call | solution.py:107
  199.0 5.6 %branch_2_fun.18 = (bf16[4,4,64,256]{3,2,1,0:T(8,128)(2,1)S(1)}, bf16[1,4,4,64,256]{4,3,2,1,0:T(8,128)(2,1)S(1)}) custom-call(s32[24]{0:T(128)S(1)} %get-tuple-element.170.order, s32[24]{0:T(128)S(1)} %get-tuple-element.171.right_dims, f32[2,16]{1,0:T(2,128)S(1)} %get-tuple-element.208.mpo, bf16[24,4,256,256]{3,2,1,0:T(8,128)(2,1)} %get-tuple-element.178.psi, ...), custom_call_target="tpu_custom_call" | custom-call | flops 1073741824 | bytes 5242880 | tf_op jit(solution)/shard_map/cond/branch_2_fun/pallas_call | solution.py:220
  206.5 4.4 %branch_2_fun.17 = (bf16[4,4,64,256]{3,2,1,0:T(8,128)(2,1)S(1)}, bf16[1,4,4,64,256]{4,3,2,1,0:T(8,128)(2,1)S(1)}) custom-call(s32[24]{0:T(128)S(1)} %get-tuple-element.170.order, s32[24]{0:T(128)S(1)} %get-tuple-element.171.right_dims, f32[2,16]{1,0:T(2,128)S(1)} %get-tuple-element.208.mpo, bf16[24,4,256,256]{3,2,1,0:T(8,128)(2,1)S(1)} %bitcast.77, ...), custom_call_target="tpu_custom_call" | custom-call | flops 1073741824 | bytes 5242880 | tf_op jit(solution)/shard_map/cond/branch_2_fun/pallas_call | solution.py:220
  211.2 9.9 %collective-permute-done.18.refs_3_ = bf16[4,256,256]{2,1,0:T(8,128)(2,1)S(1)} collective-permute-done((bf16[4,256,256]{2,1,0:T(8,128)(2,1)}, bf16[4,256,256]{2,1,0:T(8,128)(2,1)S(1)}, u32[]{:S(2)}, u32[]{:S(2)}) %collective-permute-start.18) | collective-permute-done | bytes 524320 | tf_op jit(solution)/shard_map/cond/branch_2_fun/ppermute | solution.py:288
  221.1 4.4 %branch_2_fun.16 = (bf16[4,4,64,256]{3,2,1,0:T(8,128)(2,1)S(1)}, bf16[1,4,4,64,256]{4,3,2,1,0:T(8,128)(2,1)S(1)}) custom-call(s32[24]{0:T(128)S(1)} %get-tuple-element.170.order, s32[24]{0:T(128)S(1)} %get-tuple-element.171.right_dims, f32[2,16]{1,0:T(2,128)S(1)} %get-tuple-element.208.mpo, bf16[24,4,256,256]{3,2,1,0:T(8,128)(2,1)S(1)} %bitcast.77, ...), custom_call_target="tpu_custom_call" | custom-call | flops 1073741824 | bytes 5242880 | tf_op jit(solution)/shard_map/cond/branch_2_fun/pallas_call | solution.py:220
  228.6 18.9 %collective-permute-done.23.refs_3_ = bf16[2,256,256]{2,1,0:T(8,128)(2,1)S(1)} collective-permute-done((bf16[2,256,256]{2,1,0:T(8,128)(2,1)S(1)}, bf16[2,256,256]{2,1,0:T(8,128)(2,1)S(1)}, u32[]{:S(2)}, u32[]{:S(2)}) %collective-permute-start.23) | collective-permute-done | bytes 262176 | tf_op jit(solution)/shard_map/cond/branch_2_fun/ppermute | solution.py:288
  247.5 3.5 %collective-permute-start.24 = (bf16[3,128,128]{2,1,0:T(8,128)(2,1)S(1)}, bf16[3,128,128]{2,1,0:T(8,128)(2,1)S(1)}, u32[]{:S(2)}, u32[]{:S(2)}) collective-permute-start(bf16[3,128,128]{2,1,0:T(8,128)(2,1)S(1)} %copy-done.31), channel_id=1, source_target_pairs={{0,16},{8,24},{16,0},{24,8},{1,17},{9,25},{17,1},{25,9},{2,18},{10... | collective-permute-start | bytes 294920 | tf_op jit(solution)/shard_map/cond/branch_2_fun/ppermute | solution.py:288
  255.9 6.7 %collective-permute-done.19.refs_1_ = bf16[4,4,64,256]{3,2,1,0:T(8,128)(2,1)S(1)} collective-permute-done((bf16[4,4,64,256]{3,2,1,0:T(8,128)(2,1)S(1)}, bf16[4,4,64,256]{3,2,1,0:T(8,128)(2,1)S(1)}, u32[]{:S(2)}, u32[]{:S(2)}) %collective-permute-start.19) | collective-permute-done | bytes 524320 | tf_op jit(solution)/shard_map/cond/branch_2_fun/ppermute | solution.py:292
  264.0 2.6 branch_2_fun.23
  266.7 2.6 branch_2_fun.22
  (106 shorter events, 49.4 us)
Async XLA Ops:
  3.9 9.2 %collective-permute-start.41 = (bf16[4,128,256]{2,1,0:T(8,128)(2,1)S(1)}, bf16[4,128,256]{2,1,0:T(8,128)(2,1)S(1)}, u32[]{:S(2)}, u32[]{:S(2)}) collective-permute-start(bf16[4,128,256]{2,1,0:T(8,128)(2,1)S(1)} %get-tuple-element.281), channel_id=1, source_target_pairs={{0,2},{1,3},{2,0},{3,1},{4,6},{5,7},{6,4},{7,5},{8,10},{9,11},{10,... | collective-permute-start | bytes 786440 | tf_op jit(solution)/shard_map/ppermute | solution.py:295
  6.8 21.1 %collective-permute-start.48 = (bf16[4,128,256]{2,1,0:T(8,128)(2,1)S(1)}, bf16[4,128,256]{2,1,0:T(8,128)(2,1)S(1)}, u32[]{:S(2)}, u32[]{:S(2)}) collective-permute-start(bf16[4,128,256]{2,1,0:T(8,128)(2,1)S(1)} %get-tuple-element.277), channel_id=1, source_target_pairs={{0,16},{8,24},{16,0},{24,8},{1,17},{9,25},{17,1},{25,9},{2,18},{10... | collective-permute-start | bytes 786440 | tf_op jit(solution)/shard_map/ppermute | solution.py:288
  9.5 20.0 %collective-permute-start.43 = (bf16[4,128,256]{2,1,0:T(8,128)(2,1)S(1)}, bf16[4,128,256]{2,1,0:T(8,128)(2,1)S(1)}, u32[]{:S(2)}, u32[]{:S(2)}) collective-permute-start(bf16[4,128,256]{2,1,0:T(8,128)(2,1)S(1)} %get-tuple-element.279), channel_id=1, source_target_pairs={{0,4},{1,5},{2,6},{3,7},{4,0},{5,1},{6,2},{7,3},{8,12},{9,13},{10,... | collective-permute-start | bytes 786440 | tf_op jit(solution)/shard_map/ppermute | solution.py:295
  11.0 21.4 %collective-permute-start.38 = (bf16[4,128,256]{2,1,0:T(8,128)(2,1)S(1)}, bf16[4,128,256]{2,1,0:T(8,128)(2,1)S(1)}, u32[]{:S(2)}, u32[]{:S(2)}) collective-permute-start(bf16[4,128,256]{2,1,0:T(8,128)(2,1)S(1)} %get-tuple-element.278), channel_id=1, source_target_pairs={{0,16},{8,24},{16,0},{24,8},{1,17},{9,25},{17,1},{25,9},{2,18},{10... | collective-permute-start | bytes 786440 | tf_op jit(solution)/shard_map/ppermute | solution.py:288
  13.1 38.3 %collective-permute-start.42 = (bf16[8,128,256]{2,1,0:T(8,128)(2,1)S(1)}, bf16[8,128,256]{2,1,0:T(8,128)(2,1)S(1)}, u32[]{:S(2)}, u32[]{:S(2)}) collective-permute-start(bf16[8,128,256]{2,1,0:T(8,128)(2,1)S(1)} %pad_maximum_fusion), channel_id=1, source_target_pairs={{0,4},{1,5},{2,6},{3,7},{4,0},{5,1},{6,2},{7,3},{8,12},{9,13},{10,... | collective-permute-start | bytes 1572872 | tf_op jit(solution)/shard_map/ppermute | solution.py:295
  29.5 24.2 %collective-permute-start.44 = (bf16[8,128,256]{2,1,0:T(8,128)(2,1)S(1)}, bf16[8,128,256]{2,1,0:T(8,128)(2,1)S(1)}, u32[]{:S(2)}, u32[]{:S(2)}) collective-permute-start(bf16[8,128,256]{2,1,0:T(8,128)(2,1)S(1)} %pad_maximum_fusion.1), channel_id=1, source_target_pairs={{0,2},{1,3},{2,0},{3,1},{4,6},{5,7},{6,4},{7,5},{8,10},{9,11},{10,... | collective-permute-start | bytes 1572872 | tf_op jit(solution)/shard_map/ppermute | solution.py:295
  32.4 17.7 %collective-permute-start.46 = (bf16[4,128,256]{2,1,0:T(8,128)(2,1)S(1)}, bf16[4,128,256]{2,1,0:T(8,128)(2,1)S(1)}, u32[]{:S(2)}, u32[]{:S(2)}) collective-permute-start(bf16[4,128,256]{2,1,0:T(8,128)(2,1)S(1)} %collective-permute-done.38), channel_id=1, source_target_pairs={{0,2},{1,3},{2,0},{3,1},{4,6},{5,7},{6,4},{7,5},{8,10},{9,11},{10,... | collective-permute-start | bytes 786440 | tf_op jit(solution)/shard_map/ppermute | solution.py:295
  34.4 27.2 %collective-permute-start.50 = (bf16[8,128,256]{2,1,0:T(8,128)(2,1)S(1)}, bf16[8,128,256]{2,1,0:T(8,128)(2,1)S(1)}, u32[]{:S(2)}, u32[]{:S(2)}) collective-permute-start(bf16[8,128,256]{2,1,0:T(8,128)(2,1)S(1)} %pad_maximum_fusion.3), channel_id=1, source_target_pairs={{0,2},{1,3},{2,0},{3,1},{4,6},{5,7},{6,4},{7,5},{8,10},{9,11},{10,... | collective-permute-start | bytes 1572872 | tf_op jit(solution)/shard_map/ppermute | solution.py:295
  50.1 9.2 %collective-permute-start.47 = (bf16[8,128,256]{2,1,0:T(8,128)(2,1)S(1)}, bf16[8,128,256]{2,1,0:T(8,128)(2,1)S(1)}, u32[]{:S(2)}, u32[]{:S(2)}) collective-permute-start(bf16[8,128,256]{2,1,0:T(8,128)(2,1)S(1)} %pad_maximum_fusion.2), channel_id=1, source_target_pairs={{0,4},{1,5},{2,6},{3,7},{4,0},{5,1},{6,2},{7,3},{8,12},{9,13},{10,... | collective-permute-start | bytes 1572872 | tf_op jit(solution)/shard_map/ppermute | solution.py:295
  54.5 37.9 %collective-permute-start.45 = (bf16[32,128,256]{2,1,0:T(8,128)(2,1)}, bf16[32,128,256]{2,1,0:T(8,128)(2,1)}, u32[]{:S(2)}, u32[]{:S(2)}) collective-permute-start(bf16[32,128,256]{2,1,0:T(8,128)(2,1)} %constant_dynamic-update-slice_fusion.refs_0_), channel_id=1, source_target_pairs={{0,1},{1,0},{2,3},{3,2},{4,5},{5,4},{6,7},{7,6},{8,9},{9,8},{10,11... | collective-permute-start | bytes 6291464 | tf_op jit(solution)/shard_map/ppermute | solution.py:295
  62.5 29.9 %collective-permute-start.51 = (bf16[32,128,256]{2,1,0:T(8,128)(2,1)}, bf16[32,128,256]{2,1,0:T(8,128)(2,1)}, u32[]{:S(2)}, u32[]{:S(2)}) collective-permute-start(bf16[32,128,256]{2,1,0:T(8,128)(2,1)} %constant_dynamic-update-slice_fusion.6.refs_2_), channel_id=1, source_target_pairs={{0,1},{1,0},{2,3},{3,2},{4,5},{5,4},{6,7},{7,6},{8,9},{9,8},{10,11... | collective-permute-start | bytes 6291464 | tf_op jit(solution)/shard_map/ppermute | solution.py:295
  65.4 76.9 %collective-permute-start.39 = (bf16[4,256,256]{2,1,0:T(8,128)(2,1)}, bf16[4,256,256]{2,1,0:T(8,128)(2,1)S(1)}, u32[]{:S(2)}, u32[]{:S(2)}) collective-permute-start(bf16[4,256,256]{2,1,0:T(8,128)(2,1)} %get-tuple-element.265), channel_id=1, source_target_pairs={{0,16},{8,24},{16,0},{24,8},{1,17},{9,25},{17,1},{25,9},{2,18},{10... | collective-permute-start | bytes 1572872 | tf_op jit(solution)/shard_map/ppermute | solution.py:288
  65.5 26.8 %collective-permute-start.40 = (f32[4,4]{1,0:T(4,128)S(1)}, f32[4,4]{1,0:T(4,128)S(1)}, u32[]{:S(2)}, u32[]{:S(2)}) collective-permute-start(f32[4,4]{1,0:T(4,128)S(1)} %bitcast.86), channel_id=1, source_target_pairs={{0,16},{8,24},{16,0},{24,8},{1,17},{9,25},{17,1},{25,9},{2,18},{10... | collective-permute-start | bytes 200 | tf_op jit(solution)/shard_map/ppermute | solution.py:288
  92.4 66.3 %collective-permute-start.53 = (bf16[4,256,256]{2,1,0:T(8,128)(2,1)}, bf16[4,256,256]{2,1,0:T(8,128)(2,1)S(1)}, u32[]{:S(2)}, u32[]{:S(2)}) collective-permute-start(bf16[4,256,256]{2,1,0:T(8,128)(2,1)} %get-tuple-element.275), channel_id=1, source_target_pairs={{0,16},{8,24},{16,0},{24,8},{1,17},{9,25},{17,1},{25,9},{2,18},{10... | collective-permute-start | bytes 1572872 | tf_op jit(solution)/shard_map/ppermute | solution.py:288
  148.0 13.6 %collective-permute-start.52 = (bf16[4,4,64,256]{3,2,1,0:T(8,128)(2,1)S(1)}, bf16[4,4,64,256]{3,2,1,0:T(8,128)(2,1)S(1)}, u32[]{:S(2)}, u32[]{:S(2)}) collective-permute-start(bf16[4,4,64,256]{3,2,1,0:T(8,128)(2,1)S(1)} %bitcast.58), channel_id=1, source_target_pairs={{0,8},{8,0},{16,24},{24,16},{1,9},{9,1},{17,25},{25,17},{2,10},{10... | collective-permute-start | bytes 1572872 | tf_op jit(solution)/shard_map/ppermute | solution.py:292
  162.4 44.1 %collective-permute-start.20 = (bf16[4,256,256]{2,1,0:T(8,128)(2,1)}, bf16[4,256,256]{2,1,0:T(8,128)(2,1)S(1)}, u32[]{:S(2)}, u32[]{:S(2)}) collective-permute-start(bf16[4,256,256]{2,1,0:T(8,128)(2,1)} %get-tuple-element.186), channel_id=1, source_target_pairs={{0,16},{8,24},{16,0},{24,8},{1,17},{9,25},{17,1},{25,9},{2,18},{10... | collective-permute-start | bytes 1572872 | tf_op jit(solution)/shard_map/cond/branch_2_fun/ppermute | solution.py:288
  196.5 24.6 %collective-permute-start.18 = (bf16[4,256,256]{2,1,0:T(8,128)(2,1)}, bf16[4,256,256]{2,1,0:T(8,128)(2,1)S(1)}, u32[]{:S(2)}, u32[]{:S(2)}) collective-permute-start(bf16[4,256,256]{2,1,0:T(8,128)(2,1)} %get-tuple-element.182), channel_id=1, source_target_pairs={{0,16},{8,24},{16,0},{24,8},{1,17},{9,25},{17,1},{25,9},{2,18},{10... | collective-permute-start | bytes 1572872 | tf_op jit(solution)/shard_map/cond/branch_2_fun/ppermute | solution.py:288
  204.6 46.3 %collective-permute-start.22 = (bf16[4,4,64,256]{3,2,1,0:T(8,128)(2,1)S(1)}, bf16[4,4,64,256]{3,2,1,0:T(8,128)(2,1)S(1)}, u32[]{:S(2)}, u32[]{:S(2)}) collective-permute-start(bf16[4,4,64,256]{3,2,1,0:T(8,128)(2,1)S(1)} %bitcast.53), channel_id=1, source_target_pairs={{0,8},{8,0},{16,24},{24,16},{1,9},{9,1},{17,25},{25,17},{2,10},{10... | collective-permute-start | bytes 1572872 | tf_op jit(solution)/shard_map/cond/branch_2_fun/ppermute | solution.py:292
  210.9 43.6 %collective-permute-start.21 = (bf16[4,4,64,256]{3,2,1,0:T(8,128)(2,1)S(1)}, bf16[4,4,64,256]{3,2,1,0:T(8,128)(2,1)S(1)}, u32[]{:S(2)}, u32[]{:S(2)}) collective-permute-start(bf16[4,4,64,256]{3,2,1,0:T(8,128)(2,1)S(1)} %bitcast.49), channel_id=1, source_target_pairs={{0,8},{8,0},{16,24},{24,16},{1,9},{9,1},{17,25},{25,17},{2,10},{10... | collective-permute-start | bytes 1572872 | tf_op jit(solution)/shard_map/cond/branch_2_fun/ppermute | solution.py:292
  225.5 37.1 %collective-permute-start.19 = (bf16[4,4,64,256]{3,2,1,0:T(8,128)(2,1)S(1)}, bf16[4,4,64,256]{3,2,1,0:T(8,128)(2,1)S(1)}, u32[]{:S(2)}, u32[]{:S(2)}) collective-permute-start(bf16[4,4,64,256]{3,2,1,0:T(8,128)(2,1)S(1)} %bitcast.50), channel_id=1, source_target_pairs={{0,8},{8,0},{16,24},{24,16},{1,9},{9,1},{17,25},{25,17},{2,10},{10... | collective-permute-start | bytes 1572872 | tf_op jit(solution)/shard_map/cond/branch_2_fun/ppermute | solution.py:292
  225.6 21.9 %collective-permute-start.23 = (bf16[2,256,256]{2,1,0:T(8,128)(2,1)S(1)}, bf16[2,256,256]{2,1,0:T(8,128)(2,1)S(1)}, u32[]{:S(2)}, u32[]{:S(2)}) collective-permute-start(bf16[2,256,256]{2,1,0:T(8,128)(2,1)S(1)} %copy-done.28), channel_id=1, source_target_pairs={{0,16},{8,24},{16,0},{24,8},{1,17},{9,25},{17,1},{25,9},{2,18},{10... | collective-permute-start | bytes 786440 | tf_op jit(solution)/shard_map/cond/branch_2_fun/ppermute | solution.py:288
  227.7 36.3 %collective-permute-start.26 = (bf16[3,128,128]{2,1,0:T(8,128)(2,1)S(1)}, bf16[3,128,128]{2,1,0:T(8,128)(2,1)S(1)}, u32[]{:S(2)}, u32[]{:S(2)}) collective-permute-start(bf16[3,128,128]{2,1,0:T(8,128)(2,1)S(1)} %copy-done.32), channel_id=1, source_target_pairs={{0,16},{8,24},{16,0},{24,8},{1,17},{9,25},{17,1},{25,9},{2,18},{10... | collective-permute-start | bytes 294920 | tf_op jit(solution)/shard_map/cond/branch_2_fun/ppermute | solution.py:288
  247.5 19.2 %collective-permute-start.24 = (bf16[3,128,128]{2,1,0:T(8,128)(2,1)S(1)}, bf16[3,128,128]{2,1,0:T(8,128)(2,1)S(1)}, u32[]{:S(2)}, u32[]{:S(2)}) collective-permute-start(bf16[3,128,128]{2,1,0:T(8,128)(2,1)S(1)} %copy-done.31), channel_id=1, source_target_pairs={{0,16},{8,24},{16,0},{24,8},{1,17},{9,25},{17,1},{25,9},{2,18},{10... | collective-permute-start | bytes 294920 | tf_op jit(solution)/shard_map/cond/branch_2_fun/ppermute | solution.py:288
  254.4 17.0 %collective-permute-start.28 = (bf16[2,4,64,256]{3,2,1,0:T(8,128)(2,1)S(1)}, bf16[2,4,64,256]{3,2,1,0:T(8,128)(2,1)S(1)}, u32[]{:S(2)}, u32[]{:S(2)}) collective-permute-start(bf16[2,4,64,256]{3,2,1,0:T(8,128)(2,1)S(1)} %bitcast.64), channel_id=1, source_target_pairs={{0,8},{8,0},{16,24},{24,16},{1,9},{9,1},{17,25},{25,17},{2,10},{10... | collective-permute-start | bytes 786440 | tf_op jit(solution)/shard_map/cond/branch_2_fun/ppermute | solution.py:292
  (20 other events, 190.1 us)

commit v4 on v3

--- a/solution.py
+++ b/solution.py
@@ -97,71 +97,17 @@
     )(dims, right)
 
 
-def pack_kernel(spans, order, right, *refs):
-    copy_pieces(order, right, refs[:-1], spans, refs[-1])
-
-
-def pack_call(spans, widths, order, right):
-    total = sum(span.stop - span.start for span in spans)
-    shapes = [jax.ShapeDtypeStruct((s.stop - s.start, w, w), right.dtype) for s, w in zip(spans, widths)]
-    return pl.pallas_call(
-        functools.partial(pack_kernel, spans),
-        in_specs=[SMEM, ANY],
-        out_specs=[ANY] * len(spans),
-        out_shape=shapes,
-        scratch_shapes=[pltpu.SemaphoreType.DMA((total,))],
-        cost_estimate=pl.CostEstimate(
-            flops=0, bytes_accessed=4 * sum(s.size for s in shapes), transcendentals=0
-        ),
-    )(order, right)
-
-
-def pick_kernel(hi, order, near, row, *refs):
-    sources, (*outs, sems) = refs[: 2 * hi], refs[2 * hi :]
-    blocks = order.shape[0]
-
-    def start(n, _):
-        k = order[n]
-        for i in range(hi):
-            for far in range(2):
-
-                @pl.when(near[k] == 1 - far)
-                def _():
-                    pltpu.make_async_copy(
-                        sources[2 * i + far].at[row[k]], outs[i].at[n], sems.at[i, n]
-                    ).start()
-
-        return 0
-
-    def finish(n, _):
-        for i in range(hi):
-            pltpu.make_async_copy(sources[2 * i].at[0], outs[i].at[n], sems.at[i, n]).wait()
-        return 0
-
-    lax.fori_loop(0, blocks, start, 0)
-    lax.fori_loop(0, blocks, finish, 0)
-
-
-def pick_call(hi, order, near, row, sources):
-    blocks = order.shape[0]
-    shape = (blocks,) + sources[0].shape[1:]
-    return pl.pallas_call(
-        functools.partial(pick_kernel, hi),
-        in_specs=[SMEM] * 3 + [ANY] * (2 * hi),
-        out_specs=[ANY] * hi,
-        out_shape=[jax.ShapeDtypeStruct(shape, sources[0].dtype)] * hi,
-        scratch_shapes=[pltpu.SemaphoreType.DMA((hi, blocks))],
-        cost_estimate=pl.CostEstimate(
-            flops=0, bytes_accessed=4 * hi * blocks * shape[1] * shape[2], transcendentals=0
-        ),
-    )(order, near, row, *sources)
-
-
-def block_kernel(hi, rows, narrow, first, order, right_dims, mpo, psi, *refs):
-    lefts, rights = refs[:hi], refs[hi : 2 * hi]
-    keep, send = refs[2 * hi :]
+def block_kernel(hi, rows, narrow, first, order, right_dims, is_near, row, sector, mpo, psi, *refs):
+    lefts, rights = refs[: 2 * hi - 1], refs[2 * hi - 1 : 3 * hi - 1]
+    keep, send = refs[3 * hi - 1 :]
     states = psi.shape[1]
-    stacked = jnp.concatenate([left[0] for left in lefts], axis=0)
+    k = order[pl.program_id(0) + first]
+    by_self = jnp.full(lefts[0].shape[1:], is_near[k], jnp.int32) > 0
+    stacked = jnp.concatenate(
+        [lefts[0][0]]
+        + [jnp.where(by_self, lefts[2 * i - 1][0], lefts[2 * i][0]) for i in range(1, hi)],
+        axis=0,
+    )
     parts = [
         jnp.dot(stacked, psi[0, p], preferred_element_type=jnp.float32) for p in range(states)
     ]
@@ -169,7 +115,7 @@
     for i in range(hi):
         right = rights[i][0]
         if not narrow:
-            r = right_dims[order[pl.program_id(0) + first]]
+            r = right_dims[k]
             inside = (lax.broadcasted_iota(jnp.int32, right.shape, 0) < r) & (
                 lax.broadcasted_iota(jnp.int32, right.shape, 1) < r
             )
@@ -194,7 +140,7 @@
             send[j, 0, s] = total[at : at + own].astype(send.dtype)
 
 
-def blocks_call(hi, lo, own_rows, narrow, span, order, right_dims, mpo, psi, lefts, right, others):
+def blocks_call(hi, lo, own_rows, narrow, span, scalars, mpo, psi, lefts, right, others):
     states, width = psi.shape[1], psi.shape[2]
     first, count = span.start, span.stop - span.start
     across = width // 2 if narrow else width
@@ -203,13 +149,24 @@
     def by_block(k, order, *_):
         return (order[k + first], 0, 0)
 
+    def by_sector(k, order, right_dims, is_near, row, sector, *_):
+        return (sector[order[k + first]], 0, 0)
+
+    def by_row(far):
+        def index(k, order, right_dims, is_near, row, *_):
+            block = order[k + first]
+            return (jnp.where(is_near[block] == 1 - far, row[block], 0), 0, 0)
+
+        return index
+
     grid_spec = pltpu.PrefetchScalarGridSpec(
-        num_scalar_prefetch=3,
+        num_scalar_prefetch=6,
         grid=(count,),
         in_specs=[
             pl.BlockSpec((1, states, width, across), lambda *at: by_block(*at) + (0,)),
         ]
-        + [pl.BlockSpec((1, rows, width), lambda k, *_: (k + first, 0, 0))] * hi
+        + [pl.BlockSpec((1, rows, width), by_sector)]
+        + [pl.BlockSpec((1, rows, width), by_row(far)) for _ in range(hi - 1) for far in range(2)]
         + [pl.BlockSpec((1, across, across), by_block)]
         + [pl.BlockSpec((1, across, across), lambda k, *_: (k, 0, 0))] * (hi - 1),
         out_specs=[
@@ -230,7 +187,7 @@
             bytes_accessed=count * 5 * states * width * across,
             transcendentals=0,
         ),
-    )(order, right_dims, mpo, psi, *lefts, right, *others)
+    )(*scalars, mpo, psi, *lefts, right, *others)
 
 
 def add_kernel(terms, span, order, *refs):
@@ -297,96 +254,100 @@
     def to_partners(x):
         return [over_hi(x, i) for i in range(1, hi)]
 
-    shards = left_call(hi, lo, own_rows, here[None], left_dims, left_env[0])
-    early = [slice(m * step, (m + 1) * step) for m in range(3)]
-    order, n_wide, *pieces = plan_call(early, right_dims, right)
+    pair = max(step // 2, 1)
+    early = [slice(0, pair), slice(pair, step), slice(step, 2 * step), slice(2 * step, 3 * step)]
+    fixed = early[-1].stop
+    order, n_wide, *pieces = plan_call(early + [slice(fixed, blocks)], right_dims, right)
+    mpo_now, dims_now = lax.optimization_barrier((mpo[0], left_dims, n_wide))[:2]
+    mpo_all = jnp.stack([mpo_now] + to_partners(mpo_now)).reshape(hi, states * states)
+    shards = left_call(hi, lo, own_rows, here[None], dims_now, left_env[0])
 
     bits = [1 << b for b in range(1, n_sec.bit_length() - 1)]
     cut = sectors // 2
 
-    def swap(i):
-        if i == 0:
-            return [shards[0][:cut], shards[0][cut:]]
-        return [over_hi(shards[i][:cut], i), over_hi(shards[i][cut:], i)]
-
-    def spread(parts):
-        first, second = parts
-        for bit, other in zip(bits, bits[::-1]):
+    def spread(first, second, waits):
+        for t, (bit, other) in enumerate(zip(bits, bits[::-1])):
+            if t > 0:
+                first, second = lax.optimization_barrier((first, second, waits[t - 1]))[:2]
             first = jnp.concatenate([first, over_bit(first, bit)])
             second = jnp.concatenate([second, over_bit(second, other)])
         near = jnp.concatenate([first, second])
-        return [near, over_bit(near, 1)]
+        return [near, over_bit(after(near, waits[-1]), 1)]
 
     gap = dest_owner[:, 0] ^ me
     up = sum(((gap // bit) % 2) << t for t, bit in enumerate(bits))
     down = sum(((gap // bit) % 2) << t for t, bit in enumerate(bits[::-1]))
-    near = 1 - gap % 2
+    is_near = 1 - gap % 2
     row = jnp.where(
         left_slot < cut,
         up * cut + left_slot,
         (n_sec // 2) * cut + down * (sectors - cut) + left_slot - cut,
     )
 
-    swapped = [swap(i) for i in range(hi)]
-    mpo_all = jnp.stack([mpo[0]] + to_partners(mpo[0])).reshape(hi, states * states)
-    sources = []
-    for parts in swapped:
-        sources += spread(parts)
-    moved = [to_partners(after(pieces[0], swapped[-1][0]))]
-    moved.append(to_partners(after(pieces[1], swapped[-1][1])))
-    most_wide = lax.pmax(after(n_wide, moved[0]), "sec")[0]
-    lefts = pick_call(hi, order, near, row, sources)
-
-    def compute(span, narrow, order, lefts, mpo_all, others):
+    swapped = [[over_hi(shards[i][:cut], i), over_hi(shards[i][cut:], i)] for i in range(1, hi)]
+    lefts = [lax.all_gather(shards[0], "sec", axis=0, tiled=True)]
+    moved = [to_partners(after(pieces[0], swapped))]
+    moved.append(to_partners(after(pieces[1], moved[0])))
+    moved.append(to_partners(after(pieces[2], moved[1])))
+    for first, second in swapped:
+        first, second = lax.optimization_barrier((first, second, mpo_all))[:2]
+        lefts += spread(first, second, moved[:2])
+    most_wide = lax.pmax(after(n_wide, moved[1]), "sec")[0]
+    mpo_all = after(mpo_all, most_wide)
+    scalars = (order, right_dims, is_near, row, dest_owner[:, 0] * sectors + left_slot)
+
+    def compute(span, narrow, scalars, lefts, mpo_all, others):
         return blocks_call(
-            hi, lo, own_rows, narrow, span, order, right_dims, mpo_all, psi, lefts, right, others
+            hi, lo, own_rows, narrow, span, scalars, mpo_all, psi, lefts, right, others
         )
 
     def exchange(send):
         return [over_lo(send[j - 1], j) for j in range(1, lo)]
 
-    keep, send = compute(early[0], False, order, lefts, mpo_all, moved[0])
-    terms = [keep] + exchange(send)
-
-    def run(cap, order, moved, third, lefts, mpo_all, terms):
-        spans = [(slice(a, min(a + step, cap)), False) for a in range(0, cap, step)]
+    terms = []
+    for m in range(2):
+        keep, send = compute(early[m], False, scalars, lefts, mpo_all, moved[m])
+        terms.append([keep] + exchange(send))
+
+    def run(cap, scalars, moved, pieces, lefts, mpo_all, terms):
+        order = scalars[0]
+        moved, terms = list(moved), list(terms)
+        spans = [(span, False) for span in early]
+        sends = [pieces[0]]
+        for a in range(fixed, cap, step):
+            spans.append((slice(a, min(a + step, cap)), False))
         rest = blocks - cap
         count = -(-rest // (step + 1))
         for q in range(count):
-            a, b = cap + rest * q // count, cap + rest * (q + 1) // count
-            spans.append((slice(a, b), True))
-        total = len(spans)
-        moved = list(moved)
-        moved.append(to_partners(third))
-        later = spans[3:]
-        pieces = [third] * 3
-        pieces += pack_call(
-            [s for s, _ in later], [half if n else width for _, n in later], order, right
-        )
+            spans.append((slice(cap + rest * q // count, cap + rest * (q + 1) // count), True))
+        for span, narrow in spans[len(early) :]:
+            across = half if narrow else width
+            sends.append(pieces[1][span.start - fixed : span.stop - fixed, :across, :across])
+        total, done = len(spans), len(moved)
+        for m in range(done, min(done + 2, total)):
+            moved.append(to_partners(sends[m - done]))
         shape = (blocks, states, own_rows, width)
-        terms = [terms]
-        out = add_call(shape, spans[0][0], order, terms[0], None)
-        added = 1
-        for m in range(1, total):
-            while added < m - 2:
+        out, added = None, 0
+        for m in range(len(terms), total):
+            if added < m - 1:
                 out = add_call(shape, spans[added][0], order, terms[added], out)
                 added += 1
-            mpo_now, out = lax.optimization_barrier((mpo_all, out))
-            if m + 2 < total:
-                waits = (moved[m], terms[m - 1][0]) if m > 1 else ()
-                moved.append(to_partners(after(pieces[m + 2], waits)))
-            keep, send = compute(*spans[m], order, lefts, mpo_now, moved[m])
+                mpo_now, out = lax.optimization_barrier((mpo_all, out))
+            keep, send = compute(*spans[m], scalars, lefts, mpo_now, moved[m])
             terms.append([keep] + exchange(send))
+            if len(moved) < total:
+                waits = (moved[-2], keep)
+                moved.append(to_partners(after(sends[len(moved) - done], waits)))
         for m in range(added, total):
             out = add_call(shape, spans[m][0], order, terms[m], out)
         return out
 
-    caps = sorted({max(3 * step, blocks * q // 12) for q in (7, 8, 9)} | {blocks})
+    caps = sorted({max(fixed, blocks * q // 12) for q in (7, 8, 9)} | {blocks})
     which = sum((most_wide > cap).astype(jnp.int32) for cap in caps[:-1])
     return lax.switch(
         which,
         [functools.partial(run, cap) for cap in caps],
-        order, moved, pieces[2], lefts, mpo_all, terms,
+        scalars, moved, pieces[3:], lefts, mpo_all, terms,
     )
 
 

time: 277 us -> 262 us (0.946)
  Pallas kernels: 123 us -> 95.1 us
  between operations: 2.27 us -> 15.4 us
  waiting for transfers between devices: 98.6 us -> 111 us
  local copies, waits for them, and re-layouts: 12.1 us -> 5.87 us
  starting transfers between devices: 32.7 us -> 27.8 us
    pallas_call x2 -> x0, Pallas kernels: 81.4 us -> none  [the longest x1 49.9 us: pick_call(): pl.pallas_call(functools.partial(pick_kernel, hi), in_specs=[SMEM] * 3 +...]
    pallas_call x1, Pallas kernels: 2.89 us -> 50.9 us  [plan_call(): pl.pallas_call(functools.partial(plan_kernel, spans), in_specs=[SMEM, ANY...]
    ppermute x7, waiting for transfers between devices: 10.7 us -> 44.5 us  [over_lo(): return lax.ppermute(x, 'chan', pairs)]
    ppermute x10, waiting for transfers between devices: 67.2 us -> 43.9 us  [over_hi(): return lax.ppermute(x, 'chan', pairs)]
    ppermute x10 -> x5, starting transfers between devices: 11.1 us -> 4.43 us  [over_bit(): return lax.ppermute(x, 'sec', [(i, i ^ bit) for i in range(n_sec)])]
    unnamed x23 -> x25, local copies, waits for them, and re-layouts: 8.57 us -> 3.83 us
    pallas_call x7, Pallas kernels: 27.3 us -> 30.9 us  [blocks_call(): pl.pallas_call(functools.partial(block_kernel, hi, rows, narrow, first),...]
    ppermute x10 -> x5, waiting for transfers between devices: 20.7 us -> 22.2 us  [over_bit(): return lax.ppermute(x, 'sec', [(i, i ^ bit) for i in range(n_sec)])]
  transfers between devices with their start and end apart: 27 -> 23, of which waited for: 11 -> 15; matrix products, arithmetic and copies ran while one was open for 3% -> 2% of each run, Pallas kernels for 44% -> 12%
where the time goes in v4:
time: 262 us; the launch traced here: 264 us
  waiting for transfers between devices  111 us (42%)
  Pallas kernels  95.1 us (36%)
  starting transfers between devices  27.8 us (11%)
  between operations  15.4 us (6%)
  blocking collectives  8.75 us (3%)
  local copies, waits for them, and re-layouts  5.87 us (2%)
    pallas_call x1, Pallas kernels, plan_call(): pl.pallas_call(functools.partial(plan_kernel, spans), in_specs=[SMEM, ANY...  50.9 us
    ppermute x7, waiting for transfers between devices, over_lo(): return lax.ppermute(x, 'chan', pairs)  44.5 us
    ppermute x10, waiting for transfers between devices, over_hi(): return lax.ppermute(x, 'chan', pairs)  43.9 us
    pallas_call x7, Pallas kernels, blocks_call(): pl.pallas_call(functools.partial(block_kernel, hi, rows, narrow, first),...  30.9 us
    ppermute x5, waiting for transfers between devices, over_bit(): return lax.ppermute(x, 'sec', [(i, i ^ bit) for i in range(n_sec)])  22.2 us
    ppermute x10, starting transfers between devices, over_hi(): return lax.ppermute(x, 'chan', pairs)  14.9 us
    pallas_call x7, Pallas kernels, add_call(): pl.pallas_call(functools.partial(add_kernel, len(terms), span), in_specs=...  10.1 us
    pmax x1, blocking collectives, on_device(): most_wide = lax.pmax(after(n_wide, moved[1]), 'sec')[0]  8.75 us
  transfers between devices with their start and end apart: 23, of which 15 were waited for; matrix products, arithmetic and copies ran while one was open for 2% of the time, Pallas kernels for 12%

profile of v4, /device:TPU:0, one launch (start us, length us, event | category | flops | bytes accessed | tf_op | source)
XLA Modules:
  0.0 264.1 jit_solution(969793909853238735)
XLA Ops:
  6.5 50.9 %shard_map.86 = (s32[24]{0:T(128)S(1)}, s32[1]{0:T(128)}, bf16[2,256,256]{2,1,0:T(8,128)(2,1)}, bf16[2,256,256]{2,1,0:T(8,128)(2,1)}, bf16[4,256,256]{2,1,0:T(8,...) custom-call(s32[24]{0:T(128)} %right_dims.3, bf16[24,256,256]{2,1,0:T(8,128)(2,1)} %bitcast.84), custom_call_target="tpu_custom_call" | custom-call | bytes 6291456 | tf_op jit(solution)/shard_map/pallas_call | solution.py:89
  57.5 3.3 %shard_map.87 = (bf16[8,128,256]{2,1,0:T(8,128)(2,1)}, bf16[8,128,256]{2,1,0:T(8,128)(2,1)S(1)}) custom-call(s32[1]{0:T(128)} %bitcast.22.here, s32[8]{0:T(128)S(1)} %copy-done.1, bf16[8,256,256]{2,1,0:T(8,128)(2,1)S(1)} %bitcast.50), custom_call_target="tpu_custom_call" | custom-call | flops 524288 | bytes 2097152 | tf_op jit(solution)/shard_map/pallas_call | solution.py:35
  60.8 4.1 %collective-permute-start.39 = (bf16[4,128,256]{2,1,0:T(8,128)(2,1)S(1)}, bf16[4,128,256]{2,1,0:T(8,128)(2,1)S(1)}, u32[]{:S(2)}, u32[]{:S(2)}) collective-permute-start(bf16[4,128,256]{2,1,0:T(8,128)(2,1)S(1)} %get-tuple-element.379), channel_id=1, source_target_pairs={{0,16},{8,24},{16,0},{24,8},{1,17},{9,25},{17,1},{25,9},{2,18},{10... | collective-permute-start | bytes 786440 | tf_op jit(solution)/shard_map/ppermute | solution.py:245
  67.9 20.2 %collective-permute-done.42 = f32[4,4]{1,0:T(4,128)S(1)} collective-permute-done((f32[4,4]{1,0:T(4,128)S(1)}, f32[4,4]{1,0:T(4,128)S(1)}, u32[]{:S(2)}, u32[]{:S(2)}) %collective-permute-start.42) | collective-permute-done | bytes 96 | tf_op jit(solution)/shard_map/ppermute | solution.py:245
  91.4 11.1 %collective-permute-done.43 = bf16[4,128,256]{2,1,0:T(8,128)(2,1)S(1)} collective-permute-done((bf16[4,128,256]{2,1,0:T(8,128)(2,1)S(1)}, bf16[4,128,256]{2,1,0:T(8,128)(2,1)S(1)}, u32[]{:S(2)}, u32[]{:S(2)}) %collective-permute-start.43) | collective-permute-done | bytes 262176 | tf_op jit(solution)/shard_map/ppermute | solution.py:252
  106.9 9.7 %collective-permute-done.45 = bf16[8,128,256]{2,1,0:T(8,128)(2,1)S(1)} collective-permute-done((bf16[8,128,256]{2,1,0:T(8,128)(2,1)S(1)}, bf16[8,128,256]{2,1,0:T(8,128)(2,1)S(1)}, u32[]{:S(2)}, u32[]{:S(2)}) %collective-permute-start.45) | collective-permute-done | bytes 524320 | tf_op jit(solution)/shard_map/ppermute | solution.py:252
  120.4 8.8 %pmax.7 = s32[]{:T(128)} all-reduce(s32[]{:T(128)} %bitcast.25), channel_id=1, replica_groups=mesh['chan'=4,'sec'=8] {'sec'}, use_global_device_ids=true, to_apply=%region_0.1 | all-reduce | flops 1 | bytes 8 | tf_op jit(solution)/shard_map/pmax | solution.py:295
  129.2 3.6 %shard_map.88 = (bf16[2,4,64,256]{3,2,1,0:T(8,128)(2,1)S(1)}, bf16[1,2,4,64,256]{4,3,2,1,0:T(8,128)(2,1)S(1)}) custom-call(s32[24]{0:T(128)S(1)} %get-tuple-element.352.order, s32[24]{0:T(128)S(1)} %copy-done.21, s32[24]{0:T(128)S(1)} %get-tuple-element.383.is_near, s32[24]{0:T(128)S(1)} %get-tuple-element.382.row, s32[24]{0:T(128)S(1)} %get-tuple-element.381.sector, ...), custom_call_target="tpu_custom_call" | custom-call | flops 536870912 | bytes 2621440 | tf_op jit(solution)/shard_map/pallas_call | solution.py:177
  136.5 3.6 %shard_map.89 = (bf16[2,4,64,256]{3,2,1,0:T(8,128)(2,1)}, bf16[1,2,4,64,256]{4,3,2,1,0:T(8,128)(2,1)S(1)}) custom-call(s32[24]{0:T(128)S(1)} %get-tuple-element.352.order, s32[24]{0:T(128)S(1)} %copy-done.21, s32[24]{0:T(128)S(1)} %get-tuple-element.383.is_near, s32[24]{0:T(128)S(1)} %get-tuple-element.382.row, s32[24]{0:T(128)S(1)} %get-tuple-element.381.sector, ...), custom_call_target="tpu_custom_call" | custom-call | flops 536870912 | bytes 2621440 | tf_op jit(solution)/shard_map/pallas_call | solution.py:177
  146.0 5.8 %collective-permute-done.48 = bf16[2,4,64,256]{3,2,1,0:T(8,128)(2,1)} collective-permute-done((bf16[2,4,64,256]{3,2,1,0:T(8,128)(2,1)S(1)}, bf16[2,4,64,256]{3,2,1,0:T(8,128)(2,1)}, u32[]{:S(2)}, u32[]{:S(2)}) %collective-permute-start.48) | collective-permute-done | bytes 262176 | tf_op jit(solution)/shard_map/ppermute | solution.py:249
  151.8 4.5 %collective-permute-done.50 = bf16[2,4,64,256]{3,2,1,0:T(8,128)(2,1)} collective-permute-done((bf16[2,4,64,256]{3,2,1,0:T(8,128)(2,1)S(1)}, bf16[2,4,64,256]{3,2,1,0:T(8,128)(2,1)}, u32[]{:S(2)}, u32[]{:S(2)}) %collective-permute-start.50) | collective-permute-done | bytes 262176 | tf_op jit(solution)/shard_map/ppermute | solution.py:249
  156.3 100.9 %conditional.1 = (bf16[24,4,64,256]{3,2,1,0:T(8,128)(2,1)}) conditional(s32[]{:T(128)} %clamp.3, (s32[24]{0:T(128)S(1)}, bf16[2,4,64,256]{3,2,1,0:T(8,128)(2,1)S(1)}, bf16[2,4,64,256]{3,2,1,0:T(8,128)(2,1)}, f32[2,16]{1,0:T(2,128)S(1)}, s32[24]{0:T(128)S(1)}, /*index=5*/s32[24]{0:T(128)S(1)}, s32[24]{0:T(128)S(1)}, ...), branch_computations={%region_1.2_spmd, %region_2.3_spmd, %region_3.4_spmd, %region_4.5_... | conditional | flops 5370281984 | bytes 126878256 | solution.py:347
  158.3 5.6 %branch_1_fun.13 = (bf16[4,4,64,256]{3,2,1,0:T(8,128)(2,1)S(1)}, bf16[1,4,4,64,256]{4,3,2,1,0:T(8,128)(2,1)S(1)}) custom-call(s32[24]{0:T(128)S(1)} %get-tuple-element.194.order, s32[24]{0:T(128)S(1)} %get-tuple-element.195.right_dims, s32[24]{0:T(128)S(1)} %get-tuple-element.196.is_near, s32[24]{0:T(128)S(1)} %get-tuple-element.197.row, ...), custom_call_target="tpu_custom_call" | custom-call | flops 1073741824 | bytes 5242880 | tf_op jit(solution)/shard_map/cond/branch_1_fun/pallas_call | solution.py:177
  164.0 3.6 %collective-permute-start.12 = (bf16[4,256,256]{2,1,0:T(8,128)(2,1)}, bf16[4,256,256]{2,1,0:T(8,128)(2,1)S(1)}, u32[]{:S(2)}, u32[]{:S(2)}) collective-permute-start(bf16[4,256,256]{2,1,0:T(8,128)(2,1)} %get-tuple-element.220), channel_id=1, source_target_pairs={{0,16},{8,24},{16,0},{24,8},{1,17},{9,25},{17,1},{25,9},{2,18},{10... | collective-permute-start | bytes 1572872 | tf_op jit(solution)/shard_map/cond/branch_1_fun/ppermute | solution.py:245
  169.7 17.9 %collective-permute-done.9.refs_1_ = bf16[4,4,64,256]{3,2,1,0:T(8,128)(2,1)S(1)} collective-permute-done((bf16[4,4,64,256]{3,2,1,0:T(8,128)(2,1)S(1)}, bf16[4,4,64,256]{3,2,1,0:T(8,128)(2,1)S(1)}, u32[]{:S(2)}, u32[]{:S(2)}) %collective-permute-start.9) | collective-permute-done | bytes 524320 | tf_op jit(solution)/shard_map/cond/branch_1_fun/ppermute | solution.py:249
  189.0 14.0 %collective-permute-done.12.refs_4_ = bf16[4,256,256]{2,1,0:T(8,128)(2,1)S(1)} collective-permute-done((bf16[4,256,256]{2,1,0:T(8,128)(2,1)}, bf16[4,256,256]{2,1,0:T(8,128)(2,1)S(1)}, u32[]{:S(2)}, u32[]{:S(2)}) %collective-permute-start.12) | collective-permute-done | bytes 524320 | tf_op jit(solution)/shard_map/cond/branch_1_fun/ppermute | solution.py:245
  203.1 4.5 %branch_1_fun.17 = (bf16[4,4,64,256]{3,2,1,0:T(8,128)(2,1)S(1)}, bf16[1,4,4,64,256]{4,3,2,1,0:T(8,128)(2,1)S(1)}) custom-call(s32[24]{0:T(128)S(1)} %get-tuple-element.194.order, s32[24]{0:T(128)S(1)} %get-tuple-element.195.right_dims, s32[24]{0:T(128)S(1)} %get-tuple-element.196.is_near, s32[24]{0:T(128)S(1)} %get-tuple-element.197.row, ...), custom_call_target="tpu_custom_call" | custom-call | flops 1073741824 | bytes 5242880 | tf_op jit(solution)/shard_map/cond/branch_1_fun/pallas_call | solution.py:177
  207.7 5.7 %collective-permute-done.10.refs_4_ = bf16[4,256,256]{2,1,0:T(8,128)(2,1)S(1)} collective-permute-done((bf16[4,256,256]{2,1,0:T(8,128)(2,1)}, bf16[4,256,256]{2,1,0:T(8,128)(2,1)S(1)}, u32[]{:S(2)}, u32[]{:S(2)}) %collective-permute-start.10) | collective-permute-done | bytes 524320 | tf_op jit(solution)/shard_map/cond/branch_1_fun/ppermute | solution.py:245
  213.5 4.6 %branch_1_fun.16 = (bf16[4,4,64,256]{3,2,1,0:T(8,128)(2,1)S(1)}, bf16[1,4,4,64,256]{4,3,2,1,0:T(8,128)(2,1)S(1)}) custom-call(s32[24]{0:T(128)S(1)} %get-tuple-element.194.order, s32[24]{0:T(128)S(1)} %get-tuple-element.195.right_dims, s32[24]{0:T(128)S(1)} %get-tuple-element.196.is_near, s32[24]{0:T(128)S(1)} %get-tuple-element.197.row, ...), custom_call_target="tpu_custom_call" | custom-call | flops 1073741824 | bytes 5242880 | tf_op jit(solution)/shard_map/cond/branch_1_fun/pallas_call | solution.py:177
  221.3 9.0 %collective-permute-done.13.refs_1_ = bf16[4,4,64,256]{3,2,1,0:T(8,128)(2,1)S(1)} collective-permute-done((bf16[4,4,64,256]{3,2,1,0:T(8,128)(2,1)S(1)}, bf16[4,4,64,256]{3,2,1,0:T(8,128)(2,1)S(1)}, u32[]{:S(2)}, u32[]{:S(2)}) %collective-permute-start.13) | collective-permute-done | bytes 524320 | tf_op jit(solution)/shard_map/cond/branch_1_fun/ppermute | solution.py:249
  233.0 4.4 %branch_1_fun.21 = (bf16[4,4,64,128]{3,2,1,0:T(8,128)(2,1)S(1)}, bf16[1,4,4,64,128]{4,3,2,1,0:T(8,128)(2,1)S(1)}) custom-call(s32[24]{0:T(128)S(1)} %get-tuple-element.194.order, s32[24]{0:T(128)S(1)} %get-tuple-element.195.right_dims, s32[24]{0:T(128)S(1)} %get-tuple-element.196.is_near, s32[24]{0:T(128)S(1)} %get-tuple-element.197.row, ...), custom_call_target="tpu_custom_call" | custom-call | flops 402653184 | bytes 2621440 | tf_op jit(solution)/shard_map/cond/branch_1_fun/pallas_call | solution.py:177
  237.5 3.5 %collective-permute-start.17 = (bf16[4,4,64,128]{3,2,1,0:T(8,128)(2,1)S(1)}, bf16[4,4,64,128]{3,2,1,0:T(8,128)(2,1)S(1)}, u32[]{:S(2)}, u32[]{:S(2)}) collective-permute-start(bf16[4,4,64,128]{3,2,1,0:T(8,128)(2,1)S(1)} %bitcast.70), channel_id=1, source_target_pairs={{0,8},{8,0},{16,24},{24,16},{1,9},{9,1},{17,25},{25,17},{2,10},{10... | collective-permute-start | bytes 786440 | tf_op jit(solution)/shard_map/cond/branch_1_fun/ppermute | solution.py:249
  242.9 4.5 %branch_1_fun.20 = (bf16[4,4,64,128]{3,2,1,0:T(8,128)(2,1)S(1)}, bf16[1,4,4,64,128]{4,3,2,1,0:T(8,128)(2,1)S(1)}) custom-call(s32[24]{0:T(128)S(1)} %get-tuple-element.194.order, s32[24]{0:T(128)S(1)} %get-tuple-element.195.right_dims, s32[24]{0:T(128)S(1)} %get-tuple-element.196.is_near, s32[24]{0:T(128)S(1)} %get-tuple-element.197.row, ...), custom_call_target="tpu_custom_call" | custom-call | flops 402653184 | bytes 2621440 | tf_op jit(solution)/shard_map/cond/branch_1_fun/pallas_call | solution.py:177
  248.9 6.7 %collective-permute-done.15.refs_1_ = bf16[4,4,64,128]{3,2,1,0:T(8,128)(2,1)S(1)} collective-permute-done((bf16[4,4,64,128]{3,2,1,0:T(8,128)(2,1)S(1)}, bf16[4,4,64,128]{3,2,1,0:T(8,128)(2,1)S(1)}, u32[]{:S(2)}, u32[]{:S(2)}) %collective-permute-start.15) | collective-permute-done | bytes 262176 | tf_op jit(solution)/shard_map/cond/branch_1_fun/ppermute | solution.py:249
  (92 shorter events, 38.5 us)
Async XLA Ops:
  6.5 58.5 %copy-start.22 = (f32[1,4,4]{2,1,0:T(4,128)S(1)}, f32[1,4,4]{2,1,0:T(4,128)}, u32[]{:S(2)}) copy-start(f32[1,4,4]{2,1,0:T(4,128)} %param.13) | copy-start | bytes 196
  6.5 122.6 %all-gather.2.cloned.1.call-start = ((), (), s32[]{:S(2)}) async-start(), calls=%async_computation | async-start | bytes 4718592 | tf_op jit(solution)/shard_map/all_gather | solution.py:288
  60.8 27.4 %collective-permute-start.39 = (bf16[4,128,256]{2,1,0:T(8,128)(2,1)S(1)}, bf16[4,128,256]{2,1,0:T(8,128)(2,1)S(1)}, u32[]{:S(2)}, u32[]{:S(2)}) collective-permute-start(bf16[4,128,256]{2,1,0:T(8,128)(2,1)S(1)} %get-tuple-element.379), channel_id=1, source_target_pairs={{0,16},{8,24},{16,0},{24,8},{1,17},{9,25},{17,1},{25,9},{2,18},{10... | collective-permute-start | bytes 786440 | tf_op jit(solution)/shard_map/ppermute | solution.py:245
  64.9 23.4 %collective-permute-start.38 = (bf16[4,128,256]{2,1,0:T(8,128)(2,1)S(1)}, bf16[4,128,256]{2,1,0:T(8,128)(2,1)S(1)}, u32[]{:S(2)}, u32[]{:S(2)}) collective-permute-start(bf16[4,128,256]{2,1,0:T(8,128)(2,1)S(1)} %get-tuple-element.380), channel_id=1, source_target_pairs={{0,16},{8,24},{16,0},{24,8},{1,17},{9,25},{17,1},{25,9},{2,18},{10... | collective-permute-start | bytes 786440 | tf_op jit(solution)/shard_map/ppermute | solution.py:245
  65.0 23.2 %collective-permute-start.42 = (f32[4,4]{1,0:T(4,128)S(1)}, f32[4,4]{1,0:T(4,128)S(1)}, u32[]{:S(2)}, u32[]{:S(2)}) collective-permute-start(f32[4,4]{1,0:T(4,128)S(1)} %bitcast.91), channel_id=1, source_target_pairs={{0,16},{8,24},{16,0},{24,8},{1,17},{9,25},{17,1},{25,9},{2,18},{10... | collective-permute-start | bytes 200 | tf_op jit(solution)/shard_map/ppermute | solution.py:245
  88.3 14.3 %collective-permute-start.43 = (bf16[4,128,256]{2,1,0:T(8,128)(2,1)S(1)}, bf16[4,128,256]{2,1,0:T(8,128)(2,1)S(1)}, u32[]{:S(2)}, u32[]{:S(2)}) collective-permute-start(bf16[4,128,256]{2,1,0:T(8,128)(2,1)S(1)} %collective-permute-done.38), channel_id=1, source_target_pairs={{0,2},{1,3},{2,0},{3,1},{4,6},{5,7},{6,4},{7,5},{8,10},{9,11},{10,... | collective-permute-start | bytes 786440 | tf_op jit(solution)/shard_map/ppermute | solution.py:252
  89.9 14.0 %collective-permute-start.44 = (bf16[4,128,256]{2,1,0:T(8,128)(2,1)S(1)}, bf16[4,128,256]{2,1,0:T(8,128)(2,1)S(1)}, u32[]{:S(2)}, u32[]{:S(2)}) collective-permute-start(bf16[4,128,256]{2,1,0:T(8,128)(2,1)S(1)} %collective-permute-done.39), channel_id=1, source_target_pairs={{0,4},{1,5},{2,6},{3,7},{4,0},{5,1},{6,2},{7,3},{8,12},{9,13},{10,... | collective-permute-start | bytes 786440 | tf_op jit(solution)/shard_map/ppermute | solution.py:252
  91.4 13.4 %collective-permute-start.40 = (bf16[2,256,256]{2,1,0:T(8,128)(2,1)}, bf16[2,256,256]{2,1,0:T(8,128)(2,1)S(1)}, u32[]{:S(2)}, u32[]{:S(2)}) collective-permute-start(bf16[2,256,256]{2,1,0:T(8,128)(2,1)} %get-tuple-element.349), channel_id=1, source_target_pairs={{0,16},{8,24},{16,0},{24,8},{1,17},{9,25},{17,1},{25,9},{2,18},{10... | collective-permute-start | bytes 786440 | tf_op jit(solution)/shard_map/ppermute | solution.py:245
  104.8 11.9 %collective-permute-start.45 = (bf16[8,128,256]{2,1,0:T(8,128)(2,1)S(1)}, bf16[8,128,256]{2,1,0:T(8,128)(2,1)S(1)}, u32[]{:S(2)}, u32[]{:S(2)}) collective-permute-start(bf16[8,128,256]{2,1,0:T(8,128)(2,1)S(1)} %pad_maximum_fusion), channel_id=1, source_target_pairs={{0,4},{1,5},{2,6},{3,7},{4,0},{5,1},{6,2},{7,3},{8,12},{9,13},{10,... | collective-permute-start | bytes 1572872 | tf_op jit(solution)/shard_map/ppermute | solution.py:252
  105.3 13.1 %collective-permute-start.46 = (bf16[8,128,256]{2,1,0:T(8,128)(2,1)S(1)}, bf16[8,128,256]{2,1,0:T(8,128)(2,1)S(1)}, u32[]{:S(2)}, u32[]{:S(2)}) collective-permute-start(bf16[8,128,256]{2,1,0:T(8,128)(2,1)S(1)} %pad_maximum_fusion.1), channel_id=1, source_target_pairs={{0,2},{1,3},{2,0},{3,1},{4,6},{5,7},{6,4},{7,5},{8,10},{9,11},{10,... | collective-permute-start | bytes 1572872 | tf_op jit(solution)/shard_map/ppermute | solution.py:252
  106.1 13.1 %collective-permute-start.41 = (bf16[2,256,256]{2,1,0:T(8,128)(2,1)}, bf16[2,256,256]{2,1,0:T(8,128)(2,1)S(1)}, u32[]{:S(2)}, u32[]{:S(2)}) collective-permute-start(bf16[2,256,256]{2,1,0:T(8,128)(2,1)} %get-tuple-element.350), channel_id=1, source_target_pairs={{0,16},{8,24},{16,0},{24,8},{1,17},{9,25},{17,1},{25,9},{2,18},{10... | collective-permute-start | bytes 786440 | tf_op jit(solution)/shard_map/ppermute | solution.py:245
  119.2 10.0 %collective-permute-start.47 = (bf16[32,128,256]{2,1,0:T(8,128)(2,1)}, bf16[32,128,256]{2,1,0:T(8,128)(2,1)}, u32[]{:S(2)}, u32[]{:S(2)}) collective-permute-start(bf16[32,128,256]{2,1,0:T(8,128)(2,1)} %constant_dynamic-update-slice_fusion.refs_1_), channel_id=1, source_target_pairs={{0,1},{1,0},{2,3},{3,2},{4,5},{5,4},{6,7},{7,6},{8,9},{9,8},{10,11... | collective-permute-start | bytes 6291464 | tf_op jit(solution)/shard_map/ppermute | solution.py:252
  119.2 26.8 %collective-permute-start.49 = (bf16[4,256,256]{2,1,0:T(8,128)(2,1)}, bf16[4,256,256]{2,1,0:T(8,128)(2,1)S(1)}, u32[]{:S(2)}, u32[]{:S(2)}) collective-permute-start(bf16[4,256,256]{2,1,0:T(8,128)(2,1)} %get-tuple-element.364), channel_id=1, source_target_pairs={{0,16},{8,24},{16,0},{24,8},{1,17},{9,25},{17,1},{25,9},{2,18},{10... | collective-permute-start | bytes 1572872 | tf_op jit(solution)/shard_map/ppermute | solution.py:245
  132.9 18.9 %collective-permute-start.48 = (bf16[2,4,64,256]{3,2,1,0:T(8,128)(2,1)S(1)}, bf16[2,4,64,256]{3,2,1,0:T(8,128)(2,1)}, u32[]{:S(2)}, u32[]{:S(2)}) collective-permute-start(bf16[2,4,64,256]{3,2,1,0:T(8,128)(2,1)S(1)} %bitcast.66), channel_id=1, source_target_pairs={{0,8},{8,0},{16,24},{24,16},{1,9},{9,1},{17,25},{25,17},{2,10},{10... | collective-permute-start | bytes 786440 | tf_op jit(solution)/shard_map/ppermute | solution.py:249
  140.1 16.2 %collective-permute-start.50 = (bf16[2,4,64,256]{3,2,1,0:T(8,128)(2,1)S(1)}, bf16[2,4,64,256]{3,2,1,0:T(8,128)(2,1)}, u32[]{:S(2)}, u32[]{:S(2)}) collective-permute-start(bf16[2,4,64,256]{3,2,1,0:T(8,128)(2,1)S(1)} %bitcast.68), channel_id=1, source_target_pairs={{0,8},{8,0},{16,24},{24,16},{1,9},{9,1},{17,25},{25,17},{2,10},{10... | collective-permute-start | bytes 786440 | tf_op jit(solution)/shard_map/ppermute | solution.py:249
  163.9 23.7 %collective-permute-start.9 = (bf16[4,4,64,256]{3,2,1,0:T(8,128)(2,1)S(1)}, bf16[4,4,64,256]{3,2,1,0:T(8,128)(2,1)S(1)}, u32[]{:S(2)}, u32[]{:S(2)}) collective-permute-start(bf16[4,4,64,256]{3,2,1,0:T(8,128)(2,1)S(1)} %bitcast.62), channel_id=1, source_target_pairs={{0,8},{8,0},{16,24},{24,16},{1,9},{9,1},{17,25},{25,17},{2,10},{10... | collective-permute-start | bytes 1572872 | tf_op jit(solution)/shard_map/cond/branch_1_fun/ppermute | solution.py:249
  164.0 39.1 %collective-permute-start.12 = (bf16[4,256,256]{2,1,0:T(8,128)(2,1)}, bf16[4,256,256]{2,1,0:T(8,128)(2,1)S(1)}, u32[]{:S(2)}, u32[]{:S(2)}) collective-permute-start(bf16[4,256,256]{2,1,0:T(8,128)(2,1)} %get-tuple-element.220), channel_id=1, source_target_pairs={{0,16},{8,24},{16,0},{24,8},{1,17},{9,25},{17,1},{25,9},{2,18},{10... | collective-permute-start | bytes 1572872 | tf_op jit(solution)/shard_map/cond/branch_1_fun/ppermute | solution.py:245
  168.4 45.0 %collective-permute-start.10 = (bf16[4,256,256]{2,1,0:T(8,128)(2,1)}, bf16[4,256,256]{2,1,0:T(8,128)(2,1)S(1)}, u32[]{:S(2)}, u32[]{:S(2)}) collective-permute-start(bf16[4,256,256]{2,1,0:T(8,128)(2,1)} %slice.33), channel_id=1, source_target_pairs={{0,16},{8,24},{16,0},{24,8},{1,17},{9,25},{17,1},{25,9},{2,18},{10... | collective-permute-start | bytes 1572872 | tf_op jit(solution)/shard_map/cond/branch_1_fun/ppermute | solution.py:245
  207.7 22.6 %collective-permute-start.13 = (bf16[4,4,64,256]{3,2,1,0:T(8,128)(2,1)S(1)}, bf16[4,4,64,256]{3,2,1,0:T(8,128)(2,1)S(1)}, u32[]{:S(2)}, u32[]{:S(2)}) collective-permute-start(bf16[4,4,64,256]{3,2,1,0:T(8,128)(2,1)S(1)} %bitcast.57), channel_id=1, source_target_pairs={{0,8},{8,0},{16,24},{24,16},{1,9},{9,1},{17,25},{25,17},{2,10},{10... | collective-permute-start | bytes 1572872 | tf_op jit(solution)/shard_map/cond/branch_1_fun/ppermute | solution.py:249
  218.0 23.5 %collective-permute-start.11 = (bf16[4,4,64,256]{3,2,1,0:T(8,128)(2,1)S(1)}, bf16[4,4,64,256]{3,2,1,0:T(8,128)(2,1)S(1)}, u32[]{:S(2)}, u32[]{:S(2)}) collective-permute-start(bf16[4,4,64,256]{3,2,1,0:T(8,128)(2,1)S(1)} %bitcast.52), channel_id=1, source_target_pairs={{0,8},{8,0},{16,24},{24,16},{1,9},{9,1},{17,25},{25,17},{2,10},{10... | collective-permute-start | bytes 1572872 | tf_op jit(solution)/shard_map/cond/branch_1_fun/ppermute | solution.py:249
  218.2 14.9 %collective-permute-start.16 = (bf16[4,128,128]{2,1,0:T(8,128)(2,1)S(1)}, bf16[4,128,128]{2,1,0:T(8,128)(2,1)S(1)}, u32[]{:S(2)}, u32[]{:S(2)}) collective-permute-start(bf16[4,128,128]{2,1,0:T(8,128)(2,1)S(1)} %get-tuple-element.230), channel_id=1, source_target_pairs={{0,16},{8,24},{16,0},{24,8},{1,17},{9,25},{17,1},{25,9},{2,18},{10... | collective-permute-start | bytes 393224 | tf_op jit(solution)/shard_map/cond/branch_1_fun/ppermute | solution.py:245
  221.2 21.7 %collective-permute-start.14 = (bf16[4,128,128]{2,1,0:T(8,128)(2,1)S(1)}, bf16[4,128,128]{2,1,0:T(8,128)(2,1)S(1)}, u32[]{:S(2)}, u32[]{:S(2)}) collective-permute-start(bf16[4,128,128]{2,1,0:T(8,128)(2,1)S(1)} %get-tuple-element.226), channel_id=1, source_target_pairs={{0,16},{8,24},{16,0},{24,8},{1,17},{9,25},{17,1},{25,9},{2,18},{10... | collective-permute-start | bytes 393224 | tf_op jit(solution)/shard_map/cond/branch_1_fun/ppermute | solution.py:245
  237.5 10.0 %collective-permute-start.17 = (bf16[4,4,64,128]{3,2,1,0:T(8,128)(2,1)S(1)}, bf16[4,4,64,128]{3,2,1,0:T(8,128)(2,1)S(1)}, u32[]{:S(2)}, u32[]{:S(2)}) collective-permute-start(bf16[4,4,64,128]{3,2,1,0:T(8,128)(2,1)S(1)} %bitcast.70), channel_id=1, source_target_pairs={{0,8},{8,0},{16,24},{24,16},{1,9},{9,1},{17,25},{25,17},{2,10},{10... | collective-permute-start | bytes 786440 | tf_op jit(solution)/shard_map/cond/branch_1_fun/ppermute | solution.py:249
  247.4 8.2 %collective-permute-start.15 = (bf16[4,4,64,128]{3,2,1,0:T(8,128)(2,1)S(1)}, bf16[4,4,64,128]{3,2,1,0:T(8,128)(2,1)S(1)}, u32[]{:S(2)}, u32[]{:S(2)}) collective-permute-start(bf16[4,4,64,128]{3,2,1,0:T(8,128)(2,1)S(1)} %bitcast.71), channel_id=1, source_target_pairs={{0,8},{8,0},{16,24},{24,16},{1,9},{9,1},{17,25},{25,17},{2,10},{10... | collective-permute-start | bytes 786440 | tf_op jit(solution)/shard_map/cond/branch_1_fun/ppermute | solution.py:249
  (17 other events, 391.4 us)
Sparse Core Ops, SparseCore 0:
  60.9 45.0 all-gather.1
